TPU v7x, 1024 devices: a whole 4x4x32 slice. The times are simulated.
1024 devices in a mesh: grp: 8 (over y, core), dev: 128 (over z, x).
Axes of the slice: x: 4, y: 4, z: 32, core: 2. Of those that a mesh axis runs over, the one named last changes fastest.
Arguments:
- atm_blocks: float32 [8, 128, 8, 64, 128], P('grp', 'dev'), may hold values from -6 to 6
- send_list: int32 [8, 128, 8, 2], P('grp', 'dev'), may hold values from 0 to 7
- weight_src: int32 [8, 128, 4, 8], P('grp', 'dev'), may hold values from 0 to 47
- weights: float32 [8, 128, 4, 8, 128, 128], P('grp', 'dev'), may hold values from -0.1875 to 0.1875
- ocean_nbrs: int32 [8, 128, 4, 4], P('grp', 'dev'), may hold values from 0 to 11
Outputs:
- ocean_fields: float32 [8, 128, 4, 64, 128], P('grp', 'dev')
All inputs are finite; a program needn't handle non-finite values.
Results may differ from a plain program's by a relative error of at most 0.0003.
Values sent between devices are 32-bit elements; how exact they have to be, the bound alone decides.
No kernel may reach another device: no remote copies, remote signals or barrier semaphores. Data moves between devices by JAX's collectives and lax.ppermute only.
A program may use at most 32 MiB of HBM per device.

v0:
```python
import jax
import jax.numpy as jnp
from jax import lax
from jax.sharding import PartitionSpec as P

SWEEPS = 2


def extended_2(block, sides, width):
    for axis, dim in sides:
        count = lax.axis_size(axis)
        forward = [(i, i + 1) for i in range(count - 1)]
        backward = [(target, source) for source, target in forward]
        low = lax.ppermute(
            lax.slice_in_dim(block, block.shape[dim] - width, None, axis=dim), axis, forward
        )
        high = lax.ppermute(lax.slice_in_dim(block, 0, width, axis=dim), axis, backward)
        block = jnp.concatenate([low, block, high], axis=dim)
    return block


def shards(atm_blocks, send_list, weight_src, weights, ocean_nbrs):
    atm = atm_blocks[0, 0]
    lists = send_list[0, 0]
    groups = lax.axis_size("grp")
    slots = lists.shape[1]
    feat = atm.shape[1]
    cells = atm.shape[2]
    source = weight_src[0, 0]
    picked = atm[lists.reshape(-1)]
    beside_all = extended_2(picked, (("dev", 0),), groups * slots)
    blocks = jnp.transpose(beside_all.reshape(3, groups, slots, feat, cells), (1, 0, 2, 3, 4))
    arrived = lax.all_to_all(blocks, "grp", split_axis=0, concat_axis=0, tiled=True)
    pool = arrived.reshape(groups * 3 * slots, feat, cells)
    gathered = pool[source]
    state = jnp.einsum("okfa,okaj->ofj", gathered, weights[0, 0], precision=lax.Precision.HIGHEST)
    nbrs = ocean_nbrs[0, 0]
    tiles = state.shape[0]
    for sweep in range(SWEEPS):
        extended = extended_2(state, (("dev", 0),), tiles)
        near = extended[nbrs]
        state = state + 0.15 * (jnp.sum(near, axis=1) - 4.0 * state)
    return state[None, None]


def solution(mesh):
    return jax.shard_map(
        shards,
        mesh=mesh,
        in_specs=(
            P("grp", "dev", None, None, None),
            P("grp", "dev", None, None),
            P("grp", "dev", None, None),
            P("grp", "dev", None, None, None, None),
            P("grp", "dev", None, None),
        ),
        out_specs=P("grp", "dev", None, None, None),
        check_vma=False,
    )
```

profile of v0, /device:TPU:486, one launch (start us, length us, event | category | flops | bytes accessed | tf_op | source)
XLA Modules:
  0.0 83.6 jit_solution(637474848685995235)
XLA Ops:
  0.0 0.9 %copy.10 = s32[1,1,8,2]{3,2,1,0:T(8,128)S(1)} copy(s32[1,1,8,2]{2,3,1,0:T(2,128)} %param.6) | data formatting | bytes 128 | tf_op args[1]
  1.0 1.5 %gather_fusion = f32[16,64,128]{2,1,0:T(8,128)S(1)} fusion(f32[8,64,128]{2,1,0:T(8,128)} %bitcast.35, s32[1024]{0:T(1024)S(1)} %pad_clamp_fusion.2), kind=kCustom, calls=%fused_computation | custom fusion | bytes 1048640 | tf_op jit(solution)/shard_map/gather | solution.py:30
  2.5 5.0 %collective-permute-start = (f32[16,64,128]{2,1,0:T(8,128)S(1)}, f32[16,64,128]{2,1,0:T(8,128)S(1)}, u32[]{:S(2)}, u32[]{:S(2)}) collective-permute-start(f32[16,64,128]{2,1,0:T(8,128)S(1)} %gather_fusion), channel_id=1, source_target_pairs={{0,1},{1,2},{2,3},{3,4},{4,5},{5,6},{6,7},{7,8},{8,9},{9,10},{10,1... | collective-permute-start | bytes 1572872 | tf_op jit(solution)/shard_map/ppermute | solution.py:14
  7.5 1.9 %collective-permute-start.1 = (f32[16,64,128]{2,1,0:T(8,128)S(1)}, f32[16,64,128]{2,1,0:T(8,128)S(1)}, u32[]{:S(2)}, u32[]{:S(2)}) collective-permute-start(f32[16,64,128]{2,1,0:T(8,128)S(1)} %gather_fusion), channel_id=1, source_target_pairs={{1,0},{2,1},{3,2},{4,3},{5,4},{6,5},{7,6},{8,7},{9,8},{10,9},{11,1... | collective-permute-start | bytes 1572872 | tf_op jit(solution)/shard_map/ppermute | solution.py:17
  9.4 9.2 %collective-permute-done = f32[16,64,128]{2,1,0:T(8,128)S(1)} collective-permute-done((f32[16,64,128]{2,1,0:T(8,128)S(1)}, f32[16,64,128]{2,1,0:T(8,128)S(1)}, u32[]{:S(2)}, u32[]{:S(2)}) %collective-permute-start) | collective-permute-done | bytes 524320 | tf_op jit(solution)/shard_map/ppermute | solution.py:14
  18.7 7.4 %collective-permute-done.1 = f32[16,64,128]{2,1,0:T(8,128)S(1)} collective-permute-done((f32[16,64,128]{2,1,0:T(8,128)S(1)}, f32[16,64,128]{2,1,0:T(8,128)S(1)}, u32[]{:S(2)}, u32[]{:S(2)}) %collective-permute-start.1) | collective-permute-done | bytes 524320 | tf_op jit(solution)/shard_map/ppermute | solution.py:17
  26.1 0.2 pad_maximum_fusion
  26.3 1.3 %copy.11 = f32[8,3,2,64,128]{4,3,2,1,0:T(8,128)} copy(f32[8,3,2,64,128]{4,3,2,0,1:T(8,128)S(1)} %bitcast.33) | data formatting | bytes 3145728 | tf_op jit(solution)/shard_map/transpose | solution.py:32
  27.5 4.6 %all-to-all-start = ((f32[8,3,2,64,128]{4,3,2,1,0:T(8,128)}), f32[8,3,2,64,128]{4,3,2,1,0:T(8,128)}, u32[]{:S(2)}, u32[]{:S(2)}) async-start(f32[8,3,2,64,128]{4,3,2,1,0:T(8,128)} %copy.11), calls=%async_computation | async-start | bytes 3145728 | tf_op jit(solution)/shard_map/all_to_all | solution.py:33
  32.2 21.6 %all-to-all-done = f32[8,3,2,64,128]{4,3,2,1,0:T(8,128)} async-done(((f32[8,3,2,64,128]{4,3,2,1,0:T(8,128)}), f32[8,3,2,64,128]{4,3,2,1,0:T(8,128)}, u32[]{:S(2)}, u32[]{:S(2)}) %all-to-all-start) | async-done | bytes 1572896 | tf_op jit(solution)/shard_map/all_to_all | solution.py:33
  53.8 2.0 %gather_fusion.1 = f32[32,64,128]{2,1,0:T(8,128)S(1)} fusion(f32[48,64,128]{2,1,0:T(8,128)} %bitcast.4, s32[1024]{0:T(1024)S(1)} %pad_clamp_fusion.1), kind=kCustom, calls=%fused_computation.1 | custom fusion | bytes 2097280 | tf_op jit(solution)/shard_map/gather | solution.py:35
  55.9 1.4 %fusion.2 = f32[4,64,128]{2,1,0:T(8,128)S(1)} fusion(f32[4,8,64,128]{3,2,1,0:T(8,128)S(1)} %bitcast.34, f32[1,1,4,8,128,128]{5,4,3,2,1,0:T(8,128)S(1)} %copy-done), kind=kOutput, calls=%fused_computation.7 | convolution fusion | flops 402653184 | bytes 3276800 | tf_op jit(solution)/shard_map/okfa,okaj->ofj/dot_general | solution.py:36
  57.3 1.9 %collective-permute-start.2 = (f32[4,64,128]{2,1,0:T(8,128)S(1)}, f32[4,64,128]{2,1,0:T(8,128)S(1)}, u32[]{:S(2)}, u32[]{:S(2)}) collective-permute-start(f32[4,64,128]{2,1,0:T(8,128)S(1)} %fusion.2), channel_id=1, source_target_pairs={{0,1},{1,2},{2,3},{3,4},{4,5},{5,6},{6,7},{7,8},{8,9},{9,10},{10,1... | collective-permute-start | bytes 393224 | tf_op jit(solution)/shard_map/ppermute | solution.py:14
  59.2 3.9 %collective-permute-start.3 = (f32[4,64,128]{2,1,0:T(8,128)S(1)}, f32[4,64,128]{2,1,0:T(8,128)S(1)}, u32[]{:S(2)}, u32[]{:S(2)}) collective-permute-start(f32[4,64,128]{2,1,0:T(8,128)S(1)} %fusion.2), channel_id=1, source_target_pairs={{1,0},{2,1},{3,2},{4,3},{5,4},{6,5},{7,6},{8,7},{9,8},{10,9},{11,1... | collective-permute-start | bytes 393224 | tf_op jit(solution)/shard_map/ppermute | solution.py:17
  63.1 0.1 reshape.110
  63.2 1.0 %collective-permute-done.2 = f32[4,64,128]{2,1,0:T(8,128)S(1)} collective-permute-done((f32[4,64,128]{2,1,0:T(8,128)S(1)}, f32[4,64,128]{2,1,0:T(8,128)S(1)}, u32[]{:S(2)}, u32[]{:S(2)}) %collective-permute-start.2) | collective-permute-done | bytes 131104 | tf_op jit(solution)/shard_map/ppermute | solution.py:14
  64.2 5.2 %collective-permute-done.3 = f32[4,64,128]{2,1,0:T(8,128)S(1)} collective-permute-done((f32[4,64,128]{2,1,0:T(8,128)S(1)}, f32[4,64,128]{2,1,0:T(8,128)S(1)}, u32[]{:S(2)}, u32[]{:S(2)}) %collective-permute-start.3) | collective-permute-done | bytes 131104 | tf_op jit(solution)/shard_map/ppermute | solution.py:17
  69.5 0.6 gather_fusion.2
  70.1 1.9 %collective-permute-start.4 = (f32[4,64,128]{2,1,0:T(8,128)S(1)}, f32[4,64,128]{2,1,0:T(8,128)S(1)}, u32[]{:S(2)}, u32[]{:S(2)}) collective-permute-start(f32[4,64,128]{2,1,0:T(8,128)S(1)} %multiply_add_fusion), channel_id=1, source_target_pairs={{0,1},{1,2},{2,3},{3,4},{4,5},{5,6},{6,7},{7,8},{8,9},{9,10},{10,1... | collective-permute-start | bytes 393224 | tf_op jit(solution)/shard_map/ppermute | solution.py:14
  72.1 3.9 %collective-permute-start.5 = (f32[4,64,128]{2,1,0:T(8,128)S(1)}, f32[4,64,128]{2,1,0:T(8,128)S(1)}, u32[]{:S(2)}, u32[]{:S(2)}) collective-permute-start(f32[4,64,128]{2,1,0:T(8,128)S(1)} %multiply_add_fusion), channel_id=1, source_target_pairs={{1,0},{2,1},{3,2},{4,3},{5,4},{6,5},{7,6},{8,7},{9,8},{10,9},{11,1... | collective-permute-start | bytes 393224 | tf_op jit(solution)/shard_map/ppermute | solution.py:17
  76.0 1.0 %collective-permute-done.4 = f32[4,64,128]{2,1,0:T(8,128)S(1)} collective-permute-done((f32[4,64,128]{2,1,0:T(8,128)S(1)}, f32[4,64,128]{2,1,0:T(8,128)S(1)}, u32[]{:S(2)}, u32[]{:S(2)}) %collective-permute-start.4) | collective-permute-done | bytes 131104 | tf_op jit(solution)/shard_map/ppermute | solution.py:14
  77.0 5.2 %collective-permute-done.5 = f32[4,64,128]{2,1,0:T(8,128)S(1)} collective-permute-done((f32[4,64,128]{2,1,0:T(8,128)S(1)}, f32[4,64,128]{2,1,0:T(8,128)S(1)}, u32[]{:S(2)}, u32[]{:S(2)}) %collective-permute-start.5) | collective-permute-done | bytes 131104 | tf_op jit(solution)/shard_map/ppermute | solution.py:17
  82.3 0.6 gather_fusion.3
  82.9 0.7 add_bitcast_fusion
  (19 shorter events, 0.4 us)
Async XLA Ops:
  0.0 55.9 %copy-start = (f32[1,1,4,8,128,128]{5,4,3,2,1,0:T(8,128)S(1)}, f32[1,1,4,8,128,128]{5,4,3,2,1,0:T(8,128)}, u32[]{:S(2)}) copy-start(f32[1,1,4,8,128,128]{5,4,3,2,1,0:T(8,128)} %param.8) | copy-start | bytes 6291460
  2.5 16.1 %collective-permute-start = (f32[16,64,128]{2,1,0:T(8,128)S(1)}, f32[16,64,128]{2,1,0:T(8,128)S(1)}, u32[]{:S(2)}, u32[]{:S(2)}) collective-permute-start(f32[16,64,128]{2,1,0:T(8,128)S(1)} %gather_fusion), channel_id=1, source_target_pairs={{0,1},{1,2},{2,3},{3,4},{4,5},{5,6},{6,7},{7,8},{8,9},{9,10},{10,1... | collective-permute-start | bytes 1572872 | tf_op jit(solution)/shard_map/ppermute | solution.py:14
  7.5 18.6 %collective-permute-start.1 = (f32[16,64,128]{2,1,0:T(8,128)S(1)}, f32[16,64,128]{2,1,0:T(8,128)S(1)}, u32[]{:S(2)}, u32[]{:S(2)}) collective-permute-start(f32[16,64,128]{2,1,0:T(8,128)S(1)} %gather_fusion), channel_id=1, source_target_pairs={{1,0},{2,1},{3,2},{4,3},{5,4},{6,5},{7,6},{8,7},{9,8},{10,9},{11,1... | collective-permute-start | bytes 1572872 | tf_op jit(solution)/shard_map/ppermute | solution.py:17
  27.5 4.6 %copy-start.1 = (s32[1,1,4,8]{3,2,1,0:T(4,128)S(1)}, s32[1,1,4,8]{3,2,1,0:T(4,128)}, u32[]{:S(2)}) copy-start(s32[1,1,4,8]{3,2,1,0:T(4,128)} %param.7) | copy-start | bytes 388
  27.5 26.3 %all-to-all-start = ((f32[8,3,2,64,128]{4,3,2,1,0:T(8,128)}), f32[8,3,2,64,128]{4,3,2,1,0:T(8,128)}, u32[]{:S(2)}, u32[]{:S(2)}) async-start(f32[8,3,2,64,128]{4,3,2,1,0:T(8,128)} %copy.11), calls=%async_computation | async-start | bytes 3145728 | tf_op jit(solution)/shard_map/all_to_all | solution.py:33
  55.9 7.3 %copy-start.2 = (s32[1,1,4,4]{3,2,1,0:T(4,128)S(1)}, s32[1,1,4,4]{3,2,1,0:T(4,128)}, u32[]{:S(2)}) copy-start(s32[1,1,4,4]{3,2,1,0:T(4,128)} %param.9) | copy-start | bytes 196
  57.3 6.9 %collective-permute-start.2 = (f32[4,64,128]{2,1,0:T(8,128)S(1)}, f32[4,64,128]{2,1,0:T(8,128)S(1)}, u32[]{:S(2)}, u32[]{:S(2)}) collective-permute-start(f32[4,64,128]{2,1,0:T(8,128)S(1)} %fusion.2), channel_id=1, source_target_pairs={{0,1},{1,2},{2,3},{3,4},{4,5},{5,6},{6,7},{7,8},{8,9},{9,10},{10,1... | collective-permute-start | bytes 393224 | tf_op jit(solution)/shard_map/ppermute | solution.py:14
  59.2 10.3 %collective-permute-start.3 = (f32[4,64,128]{2,1,0:T(8,128)S(1)}, f32[4,64,128]{2,1,0:T(8,128)S(1)}, u32[]{:S(2)}, u32[]{:S(2)}) collective-permute-start(f32[4,64,128]{2,1,0:T(8,128)S(1)} %fusion.2), channel_id=1, source_target_pairs={{1,0},{2,1},{3,2},{4,3},{5,4},{6,5},{7,6},{8,7},{9,8},{10,9},{11,1... | collective-permute-start | bytes 393224 | tf_op jit(solution)/shard_map/ppermute | solution.py:17
  70.1 6.9 %collective-permute-start.4 = (f32[4,64,128]{2,1,0:T(8,128)S(1)}, f32[4,64,128]{2,1,0:T(8,128)S(1)}, u32[]{:S(2)}, u32[]{:S(2)}) collective-permute-start(f32[4,64,128]{2,1,0:T(8,128)S(1)} %multiply_add_fusion), channel_id=1, source_target_pairs={{0,1},{1,2},{2,3},{3,4},{4,5},{5,6},{6,7},{7,8},{8,9},{9,10},{10,1... | collective-permute-start | bytes 393224 | tf_op jit(solution)/shard_map/ppermute | solution.py:14
  72.1 10.2 %collective-permute-start.5 = (f32[4,64,128]{2,1,0:T(8,128)S(1)}, f32[4,64,128]{2,1,0:T(8,128)S(1)}, u32[]{:S(2)}, u32[]{:S(2)}) collective-permute-start(f32[4,64,128]{2,1,0:T(8,128)S(1)} %multiply_add_fusion), channel_id=1, source_target_pairs={{1,0},{2,1},{3,2},{4,3},{5,4},{6,5},{7,6},{8,7},{9,8},{10,9},{11,1... | collective-permute-start | bytes 393224 | tf_op jit(solution)/shard_map/ppermute | solution.py:17
where the time goes:
time: 83.9 us; the launch traced here: 83.6 us
  waiting for transfers between devices  50.7 us (60%)
  starting transfers between devices  23.2 us (28%)
  local copies, waits for them, and re-layouts  7.13 us (8%)
  matrix products  1.37 us (2%)
  other arithmetic  1.03 us (1%)
    all_to_all x1, waiting for transfers between devices, shards(): lax.all_to_all(blocks, 'grp', split_axis=0, concat_axis=0, tiled=True)  21.6 us
    ppermute x3, waiting for transfers between devices, extended_2(): lax.ppermute(lax.slice_in_dim(block, 0, width, axis=dim), axis, backward)  17.9 us
    ppermute x3, waiting for transfers between devices, extended_2(): lax.ppermute(lax.slice_in_dim(block, block.shape[dim] - width, None, axis...  11.2 us
    ppermute x3, starting transfers between devices, extended_2(): lax.ppermute(lax.slice_in_dim(block, 0, width, axis=dim), axis, backward)  9.76 us
    ppermute x3, starting transfers between devices, extended_2(): lax.ppermute(lax.slice_in_dim(block, block.shape[dim] - width, None, axis...  8.79 us
    all_to_all x1, starting transfers between devices, shards(): lax.all_to_all(blocks, 'grp', split_axis=0, concat_axis=0, tiled=True)  4.6 us
    gather x1, local copies, waits for them, and re-layouts, shards(): gathered = pool[source]  2.02 us
  transfers between devices with their start and end apart: 7, of which 7 were waited for; matrix products, arithmetic and copies ran while one was open for 0% of the time, Pallas kernels for 0%

commit v1 on v0

v1 whole, which is shorter than its diff:
```python
import jax
import jax.numpy as jnp
from jax import lax
from jax.experimental import pallas as pl
from jax.experimental.pallas import tpu as pltpu
from jax.sharding import PartitionSpec as P

QUAD = 4
VMEM = pl.BlockSpec(memory_space=pltpu.VMEM)
SMEM = pl.BlockSpec(memory_space=pltpu.SMEM)
ANY = pl.BlockSpec(memory_space=pl.ANY)
PARAMS = pltpu.CompilerParams(vmem_limit_bytes=24 * 1024 * 1024)


def pick_kernel(lists, atm, out, sems):
    groups, slots = out.shape[0], out.shape[1]
    copies = []
    for g in range(groups):
        for c in range(slots):
            copy = pltpu.make_async_copy(atm.at[lists[g, c]], out.at[g, c], sems.at[g, c])
            copy.start()
            copies.append(copy)
    for copy in copies:
        copy.wait()


def pick(lists, atm):
    groups, slots = lists.shape
    shape = (groups, slots) + atm.shape[1:]
    return pl.pallas_call(
        pick_kernel,
        out_shape=jax.ShapeDtypeStruct(shape, jnp.float32),
        in_specs=[SMEM, ANY],
        out_specs=VMEM,
        scratch_shapes=[pltpu.SemaphoreType.DMA((groups, slots))],
        compiler_params=PARAMS,
        cost_estimate=pl.CostEstimate(flops=0, bytes_accessed=2 * 4 * groups * slots * 64 * 128, transcendentals=0),
        name="pick",
    )(lists, atm)


def halves(x):
    high = x.astype(jnp.bfloat16)
    return high, (x - high.astype(jnp.float32)).astype(jnp.bfloat16)


def remap_kernel(slots, source, low, own, high, weights, out):
    tiles, blocks, cells = weights.shape[0], weights.shape[1], weights.shape[3]
    feat = out.shape[2]
    for b in range(tiles):
        parts = []
        for k in range(blocks):
            p = source[b, k]
            pair = lax.div(p, slots)
            side = lax.rem(pair, 3)
            row = (lax.div(pair, 3) * slots + lax.rem(p, slots)) * feat
            rows = pl.ds(pl.multiple_of(row, feat), feat)
            parts.append(jnp.where(side == 0, low[rows, :], jnp.where(side == 1, own[rows, :], high[rows, :])))
        left = jnp.concatenate(parts, axis=1)
        left_high, left_low = halves(left)
        right_high, right_low = halves(weights[b].reshape(blocks * cells, cells))
        left = jnp.concatenate([left_high, left_low], axis=0)
        right = jnp.concatenate([right_high, right_low], axis=1)
        product = jnp.dot(left, right, preferred_element_type=jnp.float32)
        total = product[:feat, :cells] + (product[:feat, cells:] + product[feat:, :cells])
        for copy in range(out.shape[0]):
            out[copy, b] = total


def remap(source, low, own, high, weights, slots, feat):
    tiles, blocks, depth, cells = weights.shape

    def kernel(*refs):
        remap_kernel(slots, *refs)

    return pl.pallas_call(
        kernel,
        out_shape=jax.ShapeDtypeStruct((QUAD, tiles, feat, cells), jnp.float32),
        in_specs=[SMEM, VMEM, VMEM, VMEM, VMEM],
        out_specs=VMEM,
        compiler_params=PARAMS,
        cost_estimate=pl.CostEstimate(flops=8 * tiles * blocks * feat * depth * cells, bytes_accessed=2**22, transcendentals=0),
        name="remap",
    )(source, low, own, high, weights)


def smooth_kernel(place, nbrs, quad, halo, out, state, first):
    tiles = out.shape[0]
    x, last = place[0], place[1]
    before = jnp.where(x < 2, 2 * tiles, 0)
    behind = jnp.where(x < 2, 0, QUAD * tiles)
    for t in range(QUAD * tiles):
        state[before + t] = quad[t]
    for t in range(2 * tiles):
        state[behind + t] = halo[t]
    centre = before + x * tiles
    degree = nbrs.shape[2]
    for e in range(3):
        for b in range(tiles):
            mine = state[centre + (e - 1) * tiles + b]
            total = None
            for m in range(degree):
                n = nbrs[e, b, m]
                if e == 2:
                    n = jnp.where(last == 1, 3 * tiles - 1, n)
                near = state[centre + (e - 2) * tiles + n]
                total = near if total is None else total + near
            first[e * tiles + b] = mine + 0.15 * (total - 4.0 * mine)
    for b in range(tiles):
        mine = first[tiles + b]
        total = None
        for m in range(degree):
            near = first[nbrs[1, b, m]]
            total = near if total is None else total + near
        out[b] = mine + 0.15 * (total - 4.0 * mine)


def smooth(place, nbrs, quad, halo):
    tiles = nbrs.shape[1]
    feat, cells = quad.shape[1:]
    return pl.pallas_call(
        smooth_kernel,
        out_shape=jax.ShapeDtypeStruct((tiles, feat, cells), jnp.float32),
        in_specs=[SMEM, SMEM, VMEM, VMEM],
        out_specs=VMEM,
        scratch_shapes=[
            pltpu.VMEM(((QUAD + 2) * tiles, feat, cells), jnp.float32),
            pltpu.VMEM((3 * tiles, feat, cells), jnp.float32),
        ],
        compiler_params=PARAMS,
        cost_estimate=pl.CostEstimate(flops=2**20, bytes_accessed=2**20, transcendentals=0),
        name="smooth",
    )(place, nbrs, quad, halo)


def shards(atm_blocks, send_list, weight_src, weights, ocean_nbrs):
    lists = send_list[0, 0]
    nbrs = ocean_nbrs[0, 0]
    groups, slots = lists.shape
    feat, cells = atm_blocks.shape[3:]
    tiles, degree = nbrs.shape
    count = lax.axis_size("dev")
    place = lax.axis_index("dev")
    x = lax.rem(place, QUAD)

    with jax.named_scope("pool"):
        picked = pick(lists, atm_blocks[0, 0])
        arrived = lax.all_to_all(picked, "grp", split_axis=0, concat_axis=0, tiled=True)
        rows = groups * slots * feat
        listed = jnp.pad(nbrs.astype(jnp.float32).reshape(1, tiles * degree), ((0, 7), (0, cells - tiles * degree)))
        own = jnp.concatenate([arrived.reshape(rows, cells), listed], axis=0)
        forward = [(i, i + 1) for i in range(count - 1)]
        backward = [(i + 1, i) for i in range(count - 1)]
        low = lax.ppermute(own, "dev", forward)
        high = lax.ppermute(own, "dev", backward)

    with jax.named_scope("remap"):
        spread = remap(weight_src[0, 0], low, own, high, weights[0, 0], slots, feat)

    with jax.named_scope("halo"):
        rings = [[z * QUAD + i for i in range(QUAD)] for z in range(count // QUAD)]
        quad = lax.all_to_all(spread, "dev", split_axis=0, concat_axis=0, axis_index_groups=rings, tiled=True)
        edge = lax.dynamic_slice_in_dim(quad, jnp.where(x < 2, 2, 0), 2, axis=0)
        hops = []
        for i in range(count):
            target = i + QUAD if i % QUAD < 2 else i - QUAD
            if 0 <= target < count:
                hops.append((i, target))
        halo = lax.ppermute(edge, "dev", hops)

    with jax.named_scope("sweeps"):

        def listed_of(payload):
            return payload[rows, : tiles * degree].astype(jnp.int32).reshape(tiles, degree)

        around = jnp.stack([listed_of(low), nbrs, listed_of(high)])
        position = jnp.stack([x, (place == count - 1).astype(jnp.int32)]).astype(jnp.int32)
        state = smooth(position, around, quad.reshape(QUAD * tiles, feat, cells), halo.reshape(2 * tiles, feat, cells))
    return state[None, None]


def solution(mesh):
    return jax.shard_map(
        shards,
        mesh=mesh,
        in_specs=(
            P("grp", "dev", None, None, None),
            P("grp", "dev", None, None),
            P("grp", "dev", None, None),
            P("grp", "dev", None, None, None, None),
            P("grp", "dev", None, None),
        ),
        out_specs=P("grp", "dev", None, None, None),
        check_vma=False,
    )
```

time: 83.9 us -> 70.4 us (0.84)
  the two profiles are of different devices: /device:TPU:486 before, /device:TPU:6 now
where the time goes in v1:
time: 70.4 us; the launch traced here: 70 us
  waiting for transfers between devices  33.5 us (48%)
  starting transfers between devices  27.8 us (39%)
  Pallas kernels  5.75 us (8%)
  local copies, waits for them, and re-layouts  2.13 us (3%)
  other arithmetic  0.84 us (1%)
    all_to_all x1, starting transfers between devices, shards(): lax.all_to_all(spread, 'dev', split_axis=0, concat_axis=0, axis_index_gro...  14 us
    ppermute x1, waiting for transfers between devices, shards(): high = lax.ppermute(own, 'dev', backward)  9.59 us
    all_to_all x1, waiting for transfers between devices, shards(): lax.all_to_all(picked, 'grp', split_axis=0, concat_axis=0, tiled=True)  9.58 us
    ppermute x1, waiting for transfers between devices, shards(): halo = lax.ppermute(edge, 'dev', hops)  6.74 us
    all_to_all x1, waiting for transfers between devices, shards(): lax.all_to_all(spread, 'dev', split_axis=0, concat_axis=0, axis_index_gro...  6.37 us
    ppermute x1, starting transfers between devices, shards(): low = lax.ppermute(own, 'dev', forward)  5.22 us
    all_to_all x1, starting transfers between devices, shards(): lax.all_to_all(picked, 'grp', split_axis=0, concat_axis=0, tiled=True)  4.48 us
    ppermute x1, starting transfers between devices, shards(): high = lax.ppermute(own, 'dev', backward)  2.74 us
  transfers between devices with their start and end apart: 5, of which 5 were waited for; matrix products, arithmetic and copies ran while one was open for 2% of the time, Pallas kernels for 0%

profile of v1, /device:TPU:6, one launch (start us, length us, event | category | flops | bytes accessed | tf_op | source)
XLA Modules:
  0.0 70.0 jit_solution(6713072511401976572)
XLA Ops:
  0.0 0.0 copy-start
  0.0 0.9 %copy.6.lists = s32[8,2]{1,0:T(8,128)S(1)} copy(s32[8,2]{0,1:T(2,128)} %bitcast.18) | data formatting | bytes 128 | tf_op jit(solution)/shard_map/squeeze | solution.py:137
  0.9 0.9 %copy-done.1 = f32[1,1,8,64,128]{4,3,2,1,0:T(8,128)S(1)} copy-done((f32[1,1,8,64,128]{4,3,2,1,0:T(8,128)S(1)}, f32[1,1,8,64,128]{4,3,2,1,0:T(8,128)}, u32[]{:S(2)}) %copy-start.1) | copy-done | bytes 262168
  1.9 2.3 %pick.1 = f32[8,2,64,128]{3,2,1,0:T(8,128)} custom-call(s32[8,2]{1,0:T(8,128)S(1)} %copy.6.lists, f32[8,64,128]{2,1,0:T(8,128)S(1)} %bitcast.13), custom_call_target="tpu_custom_call" | custom-call | bytes 1048576 | tf_op jit(solution)/shard_map/pool/pick/pallas_call | solution.py:30
  4.2 4.5 %all-to-all-start = ((f32[8,2,64,128]{3,2,1,0:T(8,128)}), f32[8,2,64,128]{3,2,1,0:T(8,128)S(1)}, u32[]{:S(2)}, u32[]{:S(2)}) async-start(f32[8,2,64,128]{3,2,1,0:T(8,128)} %pick.1), calls=%async_computation | async-start | bytes 1048576 | tf_op jit(solution)/shard_map/pool/all_to_all | solution.py:148
  8.6 0.7 convert_element_type.42
  9.3 0.1 convert_element_type.43
  9.4 9.6 %all-to-all-done = f32[8,2,64,128]{3,2,1,0:T(8,128)S(1)} async-done(((f32[8,2,64,128]{3,2,1,0:T(8,128)}), f32[8,2,64,128]{3,2,1,0:T(8,128)S(1)}, u32[]{:S(2)}, u32[]{:S(2)}) %all-to-all-start) | async-done | bytes 524320 | tf_op jit(solution)/shard_map/pool/all_to_all | solution.py:148
  19.0 2.7 %collective-permute-start.1 = (f32[1032,128]{1,0:T(8,128)S(1)}, f32[1032,128]{1,0:T(8,128)S(1)}, u32[]{:S(2)}, u32[]{:S(2)}) collective-permute-start(f32[1032,128]{1,0:T(8,128)S(1)} %select_maximum_fusion.refs_2_), channel_id=1, source_target_pairs={{1,0},{2,1},{3,2},{4,3},{5,4},{6,5},{7,6},{8,7},{9,8},{10,9},{11,1... | collective-permute-start | bytes 1585160 | tf_op jit(solution)/shard_map/pool/ppermute | solution.py:155
  21.8 5.2 %collective-permute-start = (f32[1032,128]{1,0:T(8,128)S(1)}, f32[1032,128]{1,0:T(8,128)S(1)}, u32[]{:S(2)}, u32[]{:S(2)}) collective-permute-start(f32[1032,128]{1,0:T(8,128)S(1)} %select_maximum_fusion.refs_2_), channel_id=1, source_target_pairs={{0,1},{1,2},{2,3},{3,4},{4,5},{5,6},{6,7},{7,8},{8,9},{9,10},{10,1... | collective-permute-start | bytes 1585160 | tf_op jit(solution)/shard_map/pool/ppermute | solution.py:154
  27.0 9.6 %collective-permute-done.1.refs_3_ = f32[1032,128]{1,0:T(8,128)S(1)} collective-permute-done((f32[1032,128]{1,0:T(8,128)S(1)}, f32[1032,128]{1,0:T(8,128)S(1)}, u32[]{:S(2)}, u32[]{:S(2)}) %collective-permute-start.1) | collective-permute-done | bytes 528416 | tf_op jit(solution)/shard_map/pool/ppermute | solution.py:155
  36.6 1.2 %collective-permute-done.refs_1_ = f32[1032,128]{1,0:T(8,128)S(1)} collective-permute-done((f32[1032,128]{1,0:T(8,128)S(1)}, f32[1032,128]{1,0:T(8,128)S(1)}, u32[]{:S(2)}, u32[]{:S(2)}) %collective-permute-start) | collective-permute-done | bytes 528416 | tf_op jit(solution)/shard_map/pool/ppermute | solution.py:154
  37.8 0.0 copy-done
  37.8 0.0 copy-done.2
  37.8 2.0 %remap.1 = f32[4,4,64,128]{3,2,1,0:T(8,128)} custom-call(s32[4,8]{1,0:T(4,128)S(1)} %bitcast.15, f32[1032,128]{1,0:T(8,128)S(1)} %collective-permute-done.refs_1_, f32[1032,128]{1,0:T(8,128)S(1)} %select_maximum_fusion.refs_2_, f32[1032,128]{1,0:T(8,128)S(1)} %collective-permute-done.1.refs_3_, f32[4,8,128,128]{3,2,1,0:T(8,128)S(1)} %bitcast.12), custom_call_target="tpu_custom_call" | custom-call | flops 268435456 | bytes 4194304 | tf_op jit(solution)/shard_map/remap/remap/pallas_call | solution.py:76
  39.7 14.0 %all-to-all-start.1 = ((f32[4,4,64,128]{3,2,1,0:T(8,128)}), f32[4,4,64,128]{3,2,1,0:T(8,128)S(1)}, u32[]{:S(2)}, u32[]{:S(2)}) async-start(f32[4,4,64,128]{3,2,1,0:T(8,128)} %remap.1), calls=%async_computation.1 | async-start | bytes 1048576 | tf_op jit(solution)/shard_map/halo/all_to_all | solution.py:162
  53.8 0.1 pad_add_fusion.1.place
  53.9 6.4 %all-to-all-done.1 = f32[4,4,64,128]{3,2,1,0:T(8,128)S(1)} async-done(((f32[4,4,64,128]{3,2,1,0:T(8,128)}), f32[4,4,64,128]{3,2,1,0:T(8,128)S(1)}, u32[]{:S(2)}, u32[]{:S(2)}) %all-to-all-start.1) | async-done | bytes 524320 | tf_op jit(solution)/shard_map/halo/all_to_all | solution.py:162
  60.3 1.3 %collective-permute-start.2 = (f32[2,4,64,128]{3,2,1,0:T(8,128)S(1)}, f32[2,4,64,128]{3,2,1,0:T(8,128)S(1)}, u32[]{:S(2)}, u32[]{:S(2)}) collective-permute-start(f32[2,4,64,128]{3,2,1,0:T(8,128)S(1)} %constant_dynamic-slice_fusion), channel_id=1, source_target_pairs={{0,4},{1,5},{4,8},{5,9},{6,2},{7,3},{8,12},{9,13},{10,6},{11,7},{1... | collective-permute-start | bytes 786440 | tf_op jit(solution)/shard_map/halo/ppermute | solution.py:169
  61.6 0.1 convert_element_type.47
  61.7 0.1 convert_element_type.45
  61.8 0.0 copy-done.3
  61.8 6.7 %collective-permute-done.2 = f32[2,4,64,128]{3,2,1,0:T(8,128)S(1)} collective-permute-done((f32[2,4,64,128]{3,2,1,0:T(8,128)S(1)}, f32[2,4,64,128]{3,2,1,0:T(8,128)S(1)}, u32[]{:S(2)}, u32[]{:S(2)}) %collective-permute-start.2) | collective-permute-done | bytes 262176 | tf_op jit(solution)/shard_map/halo/ppermute | solution.py:169
  68.5 1.5 %smooth.1 = f32[4,64,128]{2,1,0:T(8,128)} custom-call(s32[2]{0:T(128)S(1)} %pad_add_fusion.1.place, s32[3,4,4]{2,1,0:T(4,128)S(1)} %pad_add_fusion.nbrs, f32[16,64,128]{2,1,0:T(8,128)S(1)} %bitcast.11, f32[8,64,128]{2,1,0:T(8,128)S(1)} %bitcast.14), custom_call_target="tpu_custom_call" | custom-call | flops 1048576 | bytes 1048576 | tf_op jit(solution)/shard_map/sweeps/smooth/pallas_call | solution.py:121
  (8 shorter events, 0.1 us)
Async XLA Ops:
  0.0 37.8 %copy-start = (f32[1,1,4,8,128,128]{5,4,3,2,1,0:T(8,128)S(1)}, f32[1,1,4,8,128,128]{5,4,3,2,1,0:T(8,128)}, u32[]{:S(2)}) copy-start(f32[1,1,4,8,128,128]{5,4,3,2,1,0:T(8,128)} %param.8) | copy-start | bytes 6291460
  0.9 0.9 %copy-start.1 = (f32[1,1,8,64,128]{4,3,2,1,0:T(8,128)S(1)}, f32[1,1,8,64,128]{4,3,2,1,0:T(8,128)}, u32[]{:S(2)}) copy-start(f32[1,1,8,64,128]{4,3,2,1,0:T(8,128)} %param.5) | copy-start | bytes 786436
  1.9 35.9 %copy-start.2 = (s32[1,1,4,8]{3,2,1,0:T(4,128)S(1)}, s32[1,1,4,8]{3,2,1,0:T(4,128)}, u32[]{:S(2)}) copy-start(s32[1,1,4,8]{3,2,1,0:T(4,128)} %param.7) | copy-start | bytes 388
  4.2 14.8 %all-to-all-start = ((f32[8,2,64,128]{3,2,1,0:T(8,128)}), f32[8,2,64,128]{3,2,1,0:T(8,128)S(1)}, u32[]{:S(2)}, u32[]{:S(2)}) async-start(f32[8,2,64,128]{3,2,1,0:T(8,128)} %pick.1), calls=%async_computation | async-start | bytes 1048576 | tf_op jit(solution)/shard_map/pool/all_to_all | solution.py:148
  19.0 17.6 %collective-permute-start.1 = (f32[1032,128]{1,0:T(8,128)S(1)}, f32[1032,128]{1,0:T(8,128)S(1)}, u32[]{:S(2)}, u32[]{:S(2)}) collective-permute-start(f32[1032,128]{1,0:T(8,128)S(1)} %select_maximum_fusion.refs_2_), channel_id=1, source_target_pairs={{1,0},{2,1},{3,2},{4,3},{5,4},{6,5},{7,6},{8,7},{9,8},{10,9},{11,1... | collective-permute-start | bytes 1585160 | tf_op jit(solution)/shard_map/pool/ppermute | solution.py:155
  21.8 16.0 %collective-permute-start = (f32[1032,128]{1,0:T(8,128)S(1)}, f32[1032,128]{1,0:T(8,128)S(1)}, u32[]{:S(2)}, u32[]{:S(2)}) collective-permute-start(f32[1032,128]{1,0:T(8,128)S(1)} %select_maximum_fusion.refs_2_), channel_id=1, source_target_pairs={{0,1},{1,2},{2,3},{3,4},{4,5},{5,6},{6,7},{7,8},{8,9},{9,10},{10,1... | collective-permute-start | bytes 1585160 | tf_op jit(solution)/shard_map/pool/ppermute | solution.py:154
  37.8 24.0 %copy-start.3 = (s32[1,1,4,4]{3,2,1,0:T(4,128)S(1)}, s32[1,1,4,4]{3,2,1,0:T(4,128)}, u32[]{:S(2)}) copy-start(s32[1,1,4,4]{3,2,1,0:T(4,128)} %param.9) | copy-start | bytes 196
  39.7 20.5 %all-to-all-start.1 = ((f32[4,4,64,128]{3,2,1,0:T(8,128)}), f32[4,4,64,128]{3,2,1,0:T(8,128)S(1)}, u32[]{:S(2)}, u32[]{:S(2)}) async-start(f32[4,4,64,128]{3,2,1,0:T(8,128)} %remap.1), calls=%async_computation.1 | async-start | bytes 1048576 | tf_op jit(solution)/shard_map/halo/all_to_all | solution.py:162
  60.3 8.3 %collective-permute-start.2 = (f32[2,4,64,128]{3,2,1,0:T(8,128)S(1)}, f32[2,4,64,128]{3,2,1,0:T(8,128)S(1)}, u32[]{:S(2)}, u32[]{:S(2)}) collective-permute-start(f32[2,4,64,128]{3,2,1,0:T(8,128)S(1)} %constant_dynamic-slice_fusion), channel_id=1, source_target_pairs={{0,4},{1,5},{4,8},{5,9},{6,2},{7,3},{8,12},{9,13},{10,6},{11,7},{1... | collective-permute-start | bytes 786440 | tf_op jit(solution)/shard_map/halo/ppermute | solution.py:169

commit v2 on v1

v2 whole, which is shorter than its diff:
```python
import functools

import jax
import jax.numpy as jnp
from jax import lax
from jax.experimental import pallas as pl
from jax.experimental.pallas import tpu as pltpu
from jax.sharding import PartitionSpec as P

QUAD = 4
VMEM = pl.BlockSpec(memory_space=pltpu.VMEM)
HBM = pl.BlockSpec(memory_space=pltpu.HBM)
PARAMS = pltpu.CompilerParams(vmem_limit_bytes=24 * 1024 * 1024)


def pick_kernel(lists, atm, out, chosen, blocks, sems):
    first = pltpu.make_async_copy(lists, chosen, sems.at[0])
    second = pltpu.make_async_copy(atm, blocks, sems.at[1])
    first.start()
    second.start()
    first.wait()
    second.wait()
    for g in range(out.shape[0]):
        for c in range(out.shape[1]):
            out[g, c] = blocks[chosen[c, g]]


def pick(lists, atm):
    slots, groups = lists.shape
    return pl.pallas_call(
        pick_kernel,
        out_shape=jax.ShapeDtypeStruct((groups, slots) + atm.shape[1:], jnp.float32),
        in_specs=[HBM, HBM],
        out_specs=VMEM,
        scratch_shapes=[
            pltpu.SMEM(lists.shape, jnp.int32),
            pltpu.VMEM(atm.shape, jnp.float32),
            pltpu.SemaphoreType.DMA((2,)),
        ],
        compiler_params=PARAMS,
        cost_estimate=pl.CostEstimate(flops=0, bytes_accessed=2**19, transcendentals=0),
        name="pick",
    )(pltpu.with_memory_space_constraint(lists, pltpu.HBM), pltpu.with_memory_space_constraint(atm, pltpu.HBM))


def halves(x):
    high = x.astype(jnp.bfloat16)
    return high, (x - high.astype(jnp.float32)).astype(jnp.bfloat16)


def split_kernel(weights, out):
    tiles, blocks, depth, cells = weights.shape
    for b in range(tiles):
        out[b] = jnp.concatenate(halves(weights[b].reshape(blocks * depth, cells)), axis=1)


def split(weights):
    tiles, blocks, depth, cells = weights.shape
    return pl.pallas_call(
        split_kernel,
        out_shape=jax.ShapeDtypeStruct((tiles, blocks * depth, 2 * cells), jnp.bfloat16),
        in_specs=[VMEM],
        out_specs=VMEM,
        compiler_params=PARAMS,
        cost_estimate=pl.CostEstimate(flops=2**20, bytes_accessed=2**22, transcendentals=0),
        name="split",
    )(weights)


def remap_kernel(slots, source, low, own, high, weights, out, pool):
    copies, tiles, feat, cells = out.shape
    entries = pool.shape[0]
    chosen = source[...]
    for side, part in enumerate((low, own, high)):
        for entry in range(entries // 3):
            s, c = divmod(entry, slots)
            pool[(s * 3 + side) * slots + c] = part[entry * feat : (entry + 1) * feat, :]
    for b in range(tiles):
        left = jnp.concatenate([pool[chosen[b, k]] for k in range(source.shape[1])], axis=1)
        left = jnp.concatenate(halves(left), axis=0)
        product = jnp.dot(left, weights[b], preferred_element_type=jnp.float32)
        total = product[:feat, :cells] + (product[:feat, cells:] + product[feat:, :cells])
        for copy in range(copies):
            out[copy, b] = total


def remap(source, low, own, high, weights, groups, slots, feat):
    tiles, depth, width = weights.shape
    cells = width // 2
    return pl.pallas_call(
        functools.partial(remap_kernel, slots),
        out_shape=jax.ShapeDtypeStruct((QUAD, tiles, feat, cells), jnp.float32),
        in_specs=[VMEM] * 5,
        out_specs=VMEM,
        scratch_shapes=[pltpu.VMEM((3 * groups * slots, feat, cells), jnp.float32)],
        compiler_params=PARAMS,
        cost_estimate=pl.CostEstimate(flops=8 * tiles * feat * depth * cells, bytes_accessed=2**22, transcendentals=0),
        name="remap",
    )(source, low, own, high, weights)


def smooth_kernel(index, quad, halo, out, state, first):
    tiles = out.shape[0]
    edge, middle = halo.shape[0], quad.shape[0]
    degree = index.shape[1] // tiles
    spot = index[...]
    for t in range(edge):
        state[t] = halo[t]
        state[edge + middle + t] = halo[t]
    for t in range(middle):
        state[edge + t] = quad[t]
    for e in range(3):
        for b in range(tiles):
            mine = state[spot[4, 0] + (e * tiles + b)]
            total = state[spot[e, b * degree]]
            for m in range(1, degree):
                total = total + state[spot[e, b * degree + m]]
            first[e * tiles + b] = mine + 0.15 * (total - 4.0 * mine)
    for b in range(tiles):
        mine = first[tiles + b]
        total = first[spot[3, b * degree]]
        for m in range(1, degree):
            total = total + first[spot[3, b * degree + m]]
        out[b] = mine + 0.15 * (total - 4.0 * mine)


def smooth(index, quad, halo):
    middle, feat, cells = quad.shape
    tiles = middle // QUAD
    edge = halo.shape[0]
    return pl.pallas_call(
        smooth_kernel,
        out_shape=jax.ShapeDtypeStruct((tiles, feat, cells), jnp.float32),
        in_specs=[VMEM, VMEM, VMEM],
        out_specs=VMEM,
        scratch_shapes=[
            pltpu.VMEM((edge + middle + edge, feat, cells), jnp.float32),
            pltpu.VMEM((3 * tiles, feat, cells), jnp.float32),
        ],
        compiler_params=PARAMS,
        cost_estimate=pl.CostEstimate(flops=2**20, bytes_accessed=2**20, transcendentals=0),
        name="smooth",
    )(index, quad, halo)


def shards(atm_blocks, send_list, weight_src, weights, ocean_nbrs):
    lists = send_list[0, 0]
    nbrs = ocean_nbrs[0, 0]
    groups, slots = lists.shape
    feat, cells = atm_blocks.shape[3:]
    tiles, degree = nbrs.shape
    count = lax.axis_size("dev")
    place = lax.axis_index("dev")
    x = lax.rem(place, QUAD)

    with jax.named_scope("pool"):
        picked = pick(lists.T, atm_blocks[0, 0])
        arrived = lax.all_to_all(picked, "grp", split_axis=0, concat_axis=0, tiled=True)
        rows = groups * slots * feat
        listed = jnp.pad(nbrs.astype(jnp.float32).reshape(1, tiles * degree), ((0, 7), (0, cells - tiles * degree)))
        own = jnp.concatenate([arrived.reshape(rows, cells), listed], axis=0)
        forward = [(i, i + 1) for i in range(count - 1)]
        backward = [(i + 1, i) for i in range(count - 1)]
        low = lax.ppermute(own, "dev", forward)
        high = lax.ppermute(own, "dev", backward)

    with jax.named_scope("remap"):
        spread = remap(weight_src[0, 0], low, own, high, split(weights[0, 0]), groups, slots, feat)

    with jax.named_scope("halo"):
        rings = [[z * QUAD + i for i in range(QUAD)] for z in range(count // QUAD)]
        quad = lax.all_to_all(spread, "dev", split_axis=0, concat_axis=0, axis_index_groups=rings, tiled=True)
        edge = lax.dynamic_slice_in_dim(quad, jnp.where(x < 2, 2, 0), 2, axis=0)
        hops = []
        for i in range(count):
            target = i + QUAD if i % QUAD < 2 else i - QUAD
            if 0 <= target < count:
                hops.append((i, target))
        halo = lax.ppermute(edge, "dev", hops)

    with jax.named_scope("sweeps"):

        def listed_of(payload):
            return payload[rows : rows + 1, : tiles * degree].astype(jnp.int32)

        centre = 2 * tiles + x * tiles
        after = jnp.where(place == count - 1, 3 * tiles - 1, listed_of(high))
        mine = nbrs.reshape(1, tiles * degree)
        index = jnp.concatenate(
            [
                listed_of(low) + (centre - 2 * tiles),
                mine + (centre - tiles),
                after + centre,
                mine,
                jnp.full((1, tiles * degree), centre - tiles, jnp.int32),
            ],
            axis=0,
        )
        state = smooth(index, quad.reshape(QUAD * tiles, feat, cells), halo.reshape(2 * tiles, feat, cells))
    return state[None, None]


def solution(mesh):
    return jax.shard_map(
        shards,
        mesh=mesh,
        in_specs=(
            P("grp", "dev", None, None, None),
            P("grp", "dev", None, None),
            P("grp", "dev", None, None),
            P("grp", "dev", None, None, None, None),
            P("grp", "dev", None, None),
        ),
        out_specs=P("grp", "dev", None, None, None),
        check_vma=False,
    )
```

time: 70.4 us -> 66.6 us (0.946)
  starting transfers between devices: 27.8 us -> 22.9 us
  waiting for transfers between devices: 33.5 us -> 38 us
  local copies, waits for them, and re-layouts: 2.13 us -> 0.82 us
  Pallas kernels: 5.75 us -> 4.45 us
  other arithmetic: 0.84 us -> 0.06 us
    ppermute x1, waiting for transfers between devices: 1.18 us -> 9.3 us  [shards(): low = lax.ppermute(own, 'dev', forward)]
    ppermute x1, waiting for transfers between devices: 9.59 us -> 5.58 us  [shards(): high = lax.ppermute(own, 'dev', backward)]
    all_to_all x1, starting transfers between devices: 14 us -> 11.3 us  [shards(): lax.all_to_all(spread, 'dev', split_axis=0, concat_axis=0, axis_index_gro...]
    ppermute x1, starting transfers between devices: 5.22 us -> 3.74 us  [shards(): low = lax.ppermute(own, 'dev', forward)]
    unnamed x8 -> x4, local copies, waits for them, and re-layouts: 0.96 us -> 0.01 us
    convert_element_type x3 -> x0, other arithmetic: 0.72 us -> none  [the longest x1 0.68 us: shards(): nbrs.astype(jnp.float32).reshape(1, tiles * degree)]
    pallas_call x2 -> x3, Pallas kernels: 4.26 us -> 3.55 us  [the longest x1 1.95 us: pick(): pl.pallas_call(pick_kernel, out_shape=jax.ShapeDtypeStruct((groups, slots...]
  transfers between devices with their start and end apart: 5 -> 5, of which waited for: 5 -> 5; matrix products, arithmetic and copies ran while one was open for 2% -> 1% of each run, Pallas kernels for 0% -> 0%
where the time goes in v2:
time: 66.6 us; the launch traced here: 66.3 us
  waiting for transfers between devices  38 us (57%)
  starting transfers between devices  22.9 us (34%)
  Pallas kernels  4.45 us (7%)
  local copies, waits for them, and re-layouts  0.82 us (1%)
    all_to_all x1, starting transfers between devices, shards(): lax.all_to_all(spread, 'dev', split_axis=0, concat_axis=0, axis_index_gro...  11.3 us
    all_to_all x1, waiting for transfers between devices, shards(): lax.all_to_all(picked, 'grp', split_axis=0, concat_axis=0, tiled=True)  9.58 us
    ppermute x1, waiting for transfers between devices, shards(): low = lax.ppermute(own, 'dev', forward)  9.3 us
    ppermute x1, waiting for transfers between devices, shards(): halo = lax.ppermute(edge, 'dev', hops)  6.9 us
    all_to_all x1, waiting for transfers between devices, shards(): lax.all_to_all(spread, 'dev', split_axis=0, concat_axis=0, axis_index_gro...  6.59 us
    ppermute x1, waiting for transfers between devices, shards(): high = lax.ppermute(own, 'dev', backward)  5.58 us
    all_to_all x1, starting transfers between devices, shards(): lax.all_to_all(picked, 'grp', split_axis=0, concat_axis=0, tiled=True)  4.48 us
    ppermute x1, starting transfers between devices, shards(): low = lax.ppermute(own, 'dev', forward)  3.74 us
  transfers between devices with their start and end apart: 5, of which 5 were waited for; matrix products, arithmetic and copies ran while one was open for 1% of the time, Pallas kernels for 0%

profile of v2, /device:TPU:6, one launch (start us, length us, event | category | flops | bytes accessed | tf_op | source)
XLA Modules:
  0.0 66.3 jit_solution(10677161133783890653)
XLA Ops:
  0.0 0.0 copy-start
  0.0 1.9 %pick.1 = f32[8,2,64,128]{3,2,1,0:T(8,128)} custom-call(s32[2,8]{1,0:T(2,128)} %bitcast.16, f32[8,64,128]{2,1,0:T(8,128)} %bitcast.15), custom_call_target="tpu_custom_call" | custom-call | bytes 524288 | tf_op jit(solution)/shard_map/pool/pick/pallas_call | solution.py:30
  2.0 4.5 %all-to-all-start = ((f32[8,2,64,128]{3,2,1,0:T(8,128)}), f32[8,2,64,128]{3,2,1,0:T(8,128)S(1)}, u32[]{:S(2)}, u32[]{:S(2)}) async-start(f32[8,2,64,128]{3,2,1,0:T(8,128)} %pick.1), calls=%async_computation | async-start | bytes 1048576 | tf_op jit(solution)/shard_map/pool/all_to_all | solution.py:158
  6.4 0.8 %squeeze.17 = s32[1,16]{1,0:T(1,128)S(1)} reshape(s32[1,1,4,4]{3,2,1,0:T(4,128)} %param.9) | data formatting | bytes 128 | tf_op jit(solution)/shard_map/squeeze | solution.py:148
  7.2 9.6 %all-to-all-done = f32[8,2,64,128]{3,2,1,0:T(8,128)S(1)} async-done(((f32[8,2,64,128]{3,2,1,0:T(8,128)}), f32[8,2,64,128]{3,2,1,0:T(8,128)S(1)}, u32[]{:S(2)}, u32[]{:S(2)}) %all-to-all-start) | async-done | bytes 524320 | tf_op jit(solution)/shard_map/pool/all_to_all | solution.py:158
  16.8 3.7 %collective-permute-start = (f32[1032,128]{1,0:T(8,128)S(1)}, f32[1032,128]{1,0:T(8,128)S(1)}, u32[]{:S(2)}, u32[]{:S(2)}) collective-permute-start(f32[1032,128]{1,0:T(8,128)S(1)} %select_maximum_fusion.own), channel_id=1, source_target_pairs={{0,1},{1,2},{2,3},{3,4},{4,5},{5,6},{6,7},{7,8},{8,9},{9,10},{10,1... | collective-permute-start | bytes 1585160 | tf_op jit(solution)/shard_map/pool/ppermute | solution.py:164
  20.6 2.1 %collective-permute-start.1 = (f32[1032,128]{1,0:T(8,128)S(1)}, f32[1032,128]{1,0:T(8,128)S(1)}, u32[]{:S(2)}, u32[]{:S(2)}) collective-permute-start(f32[1032,128]{1,0:T(8,128)S(1)} %select_maximum_fusion.own), channel_id=1, source_target_pairs={{1,0},{2,1},{3,2},{4,3},{5,4},{6,5},{7,6},{8,7},{9,8},{10,9},{11,1... | collective-permute-start | bytes 1585160 | tf_op jit(solution)/shard_map/pool/ppermute | solution.py:165
  22.7 0.0 copy-done
  22.7 0.0 copy-start.1
  22.7 0.3 split.1.weights
  23.0 9.3 %collective-permute-done.low = f32[1032,128]{1,0:T(8,128)S(1)} collective-permute-done((f32[1032,128]{1,0:T(8,128)S(1)}, f32[1032,128]{1,0:T(8,128)S(1)}, u32[]{:S(2)}, u32[]{:S(2)}) %collective-permute-start) | collective-permute-done | bytes 528416 | tf_op jit(solution)/shard_map/pool/ppermute | solution.py:164
  32.3 5.6 %collective-permute-done.1.high = f32[1032,128]{1,0:T(8,128)S(1)} collective-permute-done((f32[1032,128]{1,0:T(8,128)S(1)}, f32[1032,128]{1,0:T(8,128)S(1)}, u32[]{:S(2)}, u32[]{:S(2)}) %collective-permute-start.1) | collective-permute-done | bytes 528416 | tf_op jit(solution)/shard_map/pool/ppermute | solution.py:165
  37.9 0.0 copy-done.1
  37.9 1.3 %remap.1 = f32[4,4,64,128]{3,2,1,0:T(8,128)} custom-call(s32[4,8]{1,0:T(4,128)S(1)} %bitcast.13, f32[1032,128]{1,0:T(8,128)S(1)} %collective-permute-done.low, f32[1032,128]{1,0:T(8,128)S(1)} %select_maximum_fusion.own, f32[1032,128]{1,0:T(8,128)S(1)} %collective-permute-done.1.high, bf16[4,1024,256]{2,1,0:T(8,128)(2,1)S(1)} %split.1.weights), custom_call_target="tpu_custom_call" | custom-call | flops 268435456 | bytes 4194304 | tf_op jit(solution)/shard_map/remap/remap/pallas_call | solution.py:90
  39.2 11.3 %all-to-all-start.1 = ((f32[4,4,64,128]{3,2,1,0:T(8,128)}), f32[4,4,64,128]{3,2,1,0:T(8,128)S(1)}, u32[]{:S(2)}, u32[]{:S(2)}) async-start(f32[4,4,64,128]{3,2,1,0:T(8,128)} %remap.1), calls=%async_computation.1 | async-start | bytes 1048576 | tf_op jit(solution)/shard_map/halo/all_to_all | solution.py:172
  50.5 6.6 %all-to-all-done.1 = f32[4,4,64,128]{3,2,1,0:T(8,128)S(1)} async-done(((f32[4,4,64,128]{3,2,1,0:T(8,128)}), f32[4,4,64,128]{3,2,1,0:T(8,128)S(1)}, u32[]{:S(2)}, u32[]{:S(2)}) %all-to-all-start.1) | async-done | bytes 524320 | tf_op jit(solution)/shard_map/halo/all_to_all | solution.py:172
  57.1 1.3 %collective-permute-start.2 = (f32[2,4,64,128]{3,2,1,0:T(8,128)S(1)}, f32[2,4,64,128]{3,2,1,0:T(8,128)S(1)}, u32[]{:S(2)}, u32[]{:S(2)}) collective-permute-start(f32[2,4,64,128]{3,2,1,0:T(8,128)S(1)} %constant_dynamic-slice_fusion), channel_id=1, source_target_pairs={{0,4},{1,5},{4,8},{5,9},{6,2},{7,3},{8,12},{9,13},{10,6},{11,7},{1... | collective-permute-start | bytes 786440 | tf_op jit(solution)/shard_map/halo/ppermute | solution.py:179
  58.5 6.9 %collective-permute-done.2 = f32[2,4,64,128]{3,2,1,0:T(8,128)S(1)} collective-permute-done((f32[2,4,64,128]{3,2,1,0:T(8,128)S(1)}, f32[2,4,64,128]{3,2,1,0:T(8,128)S(1)}, u32[]{:S(2)}, u32[]{:S(2)}) %collective-permute-start.2) | collective-permute-done | bytes 262176 | tf_op jit(solution)/shard_map/halo/ppermute | solution.py:179
  65.4 0.9 %smooth.1 = f32[4,64,128]{2,1,0:T(8,128)} custom-call(s32[5,16]{1,0:T(8,128)S(1)} %concatenate.7.index, f32[16,64,128]{2,1,0:T(8,128)S(1)} %bitcast.10, f32[8,64,128]{2,1,0:T(8,128)S(1)} %bitcast.12), custom_call_target="tpu_custom_call" | custom-call | flops 1048576 | bytes 1048576 | tf_op jit(solution)/shard_map/sweeps/smooth/pallas_call | solution.py:131
  (7 shorter events, 0.1 us)
Async XLA Ops:
  0.0 22.7 %copy-start = (f32[1,1,4,8,128,128]{5,4,3,2,1,0:T(8,128)S(1)}, f32[1,1,4,8,128,128]{5,4,3,2,1,0:T(8,128)}, u32[]{:S(2)}) copy-start(f32[1,1,4,8,128,128]{5,4,3,2,1,0:T(8,128)} %param.8) | copy-start | bytes 6291460
  2.0 14.8 %all-to-all-start = ((f32[8,2,64,128]{3,2,1,0:T(8,128)}), f32[8,2,64,128]{3,2,1,0:T(8,128)S(1)}, u32[]{:S(2)}, u32[]{:S(2)}) async-start(f32[8,2,64,128]{3,2,1,0:T(8,128)} %pick.1), calls=%async_computation | async-start | bytes 1048576 | tf_op jit(solution)/shard_map/pool/all_to_all | solution.py:158
  16.8 15.4 %collective-permute-start = (f32[1032,128]{1,0:T(8,128)S(1)}, f32[1032,128]{1,0:T(8,128)S(1)}, u32[]{:S(2)}, u32[]{:S(2)}) collective-permute-start(f32[1032,128]{1,0:T(8,128)S(1)} %select_maximum_fusion.own), channel_id=1, source_target_pairs={{0,1},{1,2},{2,3},{3,4},{4,5},{5,6},{6,7},{7,8},{8,9},{9,10},{10,1... | collective-permute-start | bytes 1585160 | tf_op jit(solution)/shard_map/pool/ppermute | solution.py:164
  20.6 17.3 %collective-permute-start.1 = (f32[1032,128]{1,0:T(8,128)S(1)}, f32[1032,128]{1,0:T(8,128)S(1)}, u32[]{:S(2)}, u32[]{:S(2)}) collective-permute-start(f32[1032,128]{1,0:T(8,128)S(1)} %select_maximum_fusion.own), channel_id=1, source_target_pairs={{1,0},{2,1},{3,2},{4,3},{5,4},{6,5},{7,6},{8,7},{9,8},{10,9},{11,1... | collective-permute-start | bytes 1585160 | tf_op jit(solution)/shard_map/pool/ppermute | solution.py:165
  22.7 15.2 %copy-start.1 = (s32[1,1,4,8]{3,2,1,0:T(4,128)S(1)}, s32[1,1,4,8]{3,2,1,0:T(4,128)}, u32[]{:S(2)}) copy-start(s32[1,1,4,8]{3,2,1,0:T(4,128)} %param.7) | copy-start | bytes 388
  39.2 17.9 %all-to-all-start.1 = ((f32[4,4,64,128]{3,2,1,0:T(8,128)}), f32[4,4,64,128]{3,2,1,0:T(8,128)S(1)}, u32[]{:S(2)}, u32[]{:S(2)}) async-start(f32[4,4,64,128]{3,2,1,0:T(8,128)} %remap.1), calls=%async_computation.1 | async-start | bytes 1048576 | tf_op jit(solution)/shard_map/halo/all_to_all | solution.py:172
  57.1 8.3 %collective-permute-start.2 = (f32[2,4,64,128]{3,2,1,0:T(8,128)S(1)}, f32[2,4,64,128]{3,2,1,0:T(8,128)S(1)}, u32[]{:S(2)}, u32[]{:S(2)}) collective-permute-start(f32[2,4,64,128]{3,2,1,0:T(8,128)S(1)} %constant_dynamic-slice_fusion), channel_id=1, source_target_pairs={{0,4},{1,5},{4,8},{5,9},{6,2},{7,3},{8,12},{9,13},{10,6},{11,7},{1... | collective-permute-start | bytes 786440 | tf_op jit(solution)/shard_map/halo/ppermute | solution.py:179

commit v3 on v2

--- a/solution.py
+++ b/solution.py
@@ -13,25 +13,26 @@
 PARAMS = pltpu.CompilerParams(vmem_limit_bytes=24 * 1024 * 1024)
 
 
-def pick_kernel(lists, atm, out, chosen, blocks, sems):
+def pick_kernel(lists, atm, *rest):
+    outs, (chosen, blocks, sems) = rest[:-3], rest[-3:]
     first = pltpu.make_async_copy(lists, chosen, sems.at[0])
     second = pltpu.make_async_copy(atm, blocks, sems.at[1])
     first.start()
     second.start()
     first.wait()
     second.wait()
-    for g in range(out.shape[0]):
-        for c in range(out.shape[1]):
-            out[g, c] = blocks[chosen[c, g]]
+    for c, out in enumerate(outs):
+        for g in range(out.shape[0]):
+            out[g] = blocks[chosen[c, g]]
 
 
 def pick(lists, atm):
     slots, groups = lists.shape
     return pl.pallas_call(
         pick_kernel,
-        out_shape=jax.ShapeDtypeStruct((groups, slots) + atm.shape[1:], jnp.float32),
+        out_shape=[jax.ShapeDtypeStruct((groups,) + atm.shape[1:], jnp.float32)] * slots,
         in_specs=[HBM, HBM],
-        out_specs=VMEM,
+        out_specs=[VMEM] * slots,
         scratch_shapes=[
             pltpu.SMEM(lists.shape, jnp.int32),
             pltpu.VMEM(atm.shape, jnp.float32),
@@ -67,14 +68,13 @@
     )(weights)
 
 
-def remap_kernel(slots, source, low, own, high, weights, out, pool):
+def remap_kernel(slots, source, *rest):
+    parts, (weights, out, pool) = rest[:-3], rest[-3:]
     copies, tiles, feat, cells = out.shape
-    entries = pool.shape[0]
     chosen = source[...]
-    for side, part in enumerate((low, own, high)):
-        for entry in range(entries // 3):
-            s, c = divmod(entry, slots)
-            pool[(s * 3 + side) * slots + c] = part[entry * feat : (entry + 1) * feat, :]
+    for at, part in enumerate(parts):
+        for s in range(pool.shape[0] // (3 * slots)):
+            pool[s * 3 * slots + at] = part[s * feat : (s + 1) * feat, :]
     for b in range(tiles):
         left = jnp.concatenate([pool[chosen[b, k]] for k in range(source.shape[1])], axis=1)
         left = jnp.concatenate(halves(left), axis=0)
@@ -84,19 +84,19 @@
             out[copy, b] = total
 
 
-def remap(source, low, own, high, weights, groups, slots, feat):
+def remap(source, parts, weights, groups, feat):
     tiles, depth, width = weights.shape
     cells = width // 2
     return pl.pallas_call(
-        functools.partial(remap_kernel, slots),
+        functools.partial(remap_kernel, len(parts) // 3),
         out_shape=jax.ShapeDtypeStruct((QUAD, tiles, feat, cells), jnp.float32),
-        in_specs=[VMEM] * 5,
+        in_specs=[VMEM] * (len(parts) + 2),
         out_specs=VMEM,
-        scratch_shapes=[pltpu.VMEM((3 * groups * slots, feat, cells), jnp.float32)],
+        scratch_shapes=[pltpu.VMEM((groups * len(parts), feat, cells), jnp.float32)],
         compiler_params=PARAMS,
         cost_estimate=pl.CostEstimate(flops=8 * tiles * feat * depth * cells, bytes_accessed=2**22, transcendentals=0),
         name="remap",
-    )(source, low, own, high, weights)
+    )(source, *parts, weights)
 
 
 def smooth_kernel(index, quad, halo, out, state, first):
@@ -155,17 +155,20 @@
 
     with jax.named_scope("pool"):
         picked = pick(lists.T, atm_blocks[0, 0])
-        arrived = lax.all_to_all(picked, "grp", split_axis=0, concat_axis=0, tiled=True)
-        rows = groups * slots * feat
         listed = jnp.pad(nbrs.astype(jnp.float32).reshape(1, tiles * degree), ((0, 7), (0, cells - tiles * degree)))
-        own = jnp.concatenate([arrived.reshape(rows, cells), listed], axis=0)
         forward = [(i, i + 1) for i in range(count - 1)]
         backward = [(i + 1, i) for i in range(count - 1)]
-        low = lax.ppermute(own, "dev", forward)
-        high = lax.ppermute(own, "dev", backward)
+        low, own, high = [], [], []
+        for c in range(slots):
+            arrived = lax.all_to_all(picked[c], "grp", split_axis=0, concat_axis=0, tiled=True)
+            arrived = arrived.reshape(groups * feat, cells)
+            own.append(jnp.concatenate([arrived, listed], axis=0) if c == 0 else arrived)
+        for c in range(slots):
+            low.append(lax.ppermute(own[c], "dev", forward))
+            high.append(lax.ppermute(own[c], "dev", backward))
 
     with jax.named_scope("remap"):
-        spread = remap(weight_src[0, 0], low, own, high, split(weights[0, 0]), groups, slots, feat)
+        spread = remap(weight_src[0, 0], low + own + high, split(weights[0, 0]), groups, feat)
 
     with jax.named_scope("halo"):
         rings = [[z * QUAD + i for i in range(QUAD)] for z in range(count // QUAD)]
@@ -181,14 +184,14 @@
     with jax.named_scope("sweeps"):
 
         def listed_of(payload):
-            return payload[rows : rows + 1, : tiles * degree].astype(jnp.int32)
+            return payload[groups * feat : groups * feat + 1, : tiles * degree].astype(jnp.int32)
 
         centre = 2 * tiles + x * tiles
-        after = jnp.where(place == count - 1, 3 * tiles - 1, listed_of(high))
+        after = jnp.where(place == count - 1, 3 * tiles - 1, listed_of(high[0]))
         mine = nbrs.reshape(1, tiles * degree)
         index = jnp.concatenate(
             [
-                listed_of(low) + (centre - 2 * tiles),
+                listed_of(low[0]) + (centre - 2 * tiles),
                 mine + (centre - tiles),
                 after + centre,
                 mine,

time: 66.6 us -> 68.5 us (1.029)
  starting transfers between devices: 22.9 us -> 31.5 us
  waiting for transfers between devices: 38 us -> 29.6 us
  local copies, waits for them, and re-layouts: 0.82 us -> 2.4 us
    ppermute x2 -> x4, waiting for transfers between devices: 14.9 us -> 7.96 us  [the longest x2 6.23 us: shards(): high.append(lax.ppermute(own[c], 'dev', backward))]
    ppermute x2 -> x4, starting transfers between devices: 5.84 us -> 12.1 us  [the longest x2 8.1 us: shards(): low.append(lax.ppermute(own[c], 'dev', forward))]
    all_to_all x1 -> x2, starting transfers between devices: 4.48 us -> 7.89 us  [shards(): lax.all_to_all(picked[c], 'grp', split_axis=0, concat_axis=0, tiled=True)]
    unnamed x4, local copies, waits for them, and re-layouts: 0.01 us -> 1.59 us
    all_to_all x1 -> x2, waiting for transfers between devices: 9.58 us -> 8.31 us  [shards(): lax.all_to_all(picked[c], 'grp', split_axis=0, concat_axis=0, tiled=True)]
    all_to_all x1, starting transfers between devices: 11.3 us -> 10.2 us  [shards(): lax.all_to_all(spread, 'dev', split_axis=0, concat_axis=0, axis_index_gro...]
  transfers between devices with their start and end apart: 5 -> 8, of which waited for: 5 -> 6; matrix products, arithmetic and copies ran while one was open for 1% -> 1% of each run, Pallas kernels for 0% -> 0%
where the time goes in v3:
time: 68.5 us; the launch traced here: 68 us
  starting transfers between devices  31.5 us (46%)
  waiting for transfers between devices  29.6 us (43%)
  Pallas kernels  4.29 us (6%)
  local copies, waits for them, and re-layouts  2.4 us (4%)
    all_to_all x1, starting transfers between devices, shards(): lax.all_to_all(spread, 'dev', split_axis=0, concat_axis=0, axis_index_gro...  10.2 us
    all_to_all x2, waiting for transfers between devices, shards(): lax.all_to_all(picked[c], 'grp', split_axis=0, concat_axis=0, tiled=True)  8.31 us
    ppermute x2, starting transfers between devices, shards(): low.append(lax.ppermute(own[c], 'dev', forward))  8.1 us
    all_to_all x2, starting transfers between devices, shards(): lax.all_to_all(picked[c], 'grp', split_axis=0, concat_axis=0, tiled=True)  7.89 us
    ppermute x1, waiting for transfers between devices, shards(): halo = lax.ppermute(edge, 'dev', hops)  6.9 us
    all_to_all x1, waiting for transfers between devices, shards(): lax.all_to_all(spread, 'dev', split_axis=0, concat_axis=0, axis_index_gro...  6.45 us
    ppermute x2, waiting for transfers between devices, shards(): high.append(lax.ppermute(own[c], 'dev', backward))  6.23 us
    ppermute x2, starting transfers between devices, shards(): high.append(lax.ppermute(own[c], 'dev', backward))  4.02 us
  transfers between devices with their start and end apart: 8, of which 6 were waited for; matrix products, arithmetic and copies ran while one was open for 1% of the time, Pallas kernels for 0%

profile of v3, /device:TPU:6, one launch (start us, length us, event | category | flops | bytes accessed | tf_op | source)
XLA Modules:
  0.0 68.0 jit_solution(17742592347730863740)
XLA Ops:
  0.0 1.8 %pick.1 = (f32[8,64,128]{2,1,0:T(8,128)}, f32[8,64,128]{2,1,0:T(8,128)}) custom-call(s32[2,8]{1,0:T(2,128)} %bitcast.20, f32[8,64,128]{2,1,0:T(8,128)} %bitcast.19), custom_call_target="tpu_custom_call" | custom-call | bytes 524288 | tf_op jit(solution)/shard_map/pool/pick/pallas_call | solution.py:31
  1.8 4.5 %all-to-all-start = ((f32[8,64,128]{2,1,0:T(8,128)}), f32[8,64,128]{2,1,0:T(8,128)S(1)}, u32[]{:S(2)}, u32[]{:S(2)}) async-start(f32[8,64,128]{2,1,0:T(8,128)} %get-tuple-element.7), calls=%async_computation | async-start | bytes 524288 | tf_op jit(solution)/shard_map/pool/all_to_all | solution.py:163
  6.3 0.8 %squeeze.17 = s32[1,16]{1,0:T(1,128)S(1)} reshape(s32[1,1,4,4]{3,2,1,0:T(4,128)} %param.9) | data formatting | bytes 128 | tf_op jit(solution)/shard_map/squeeze | solution.py:148
  7.0 6.8 %all-to-all-done = f32[8,64,128]{2,1,0:T(8,128)S(1)} async-done(((f32[8,64,128]{2,1,0:T(8,128)}), f32[8,64,128]{2,1,0:T(8,128)S(1)}, u32[]{:S(2)}, u32[]{:S(2)}) %all-to-all-start) | async-done | bytes 262176 | tf_op jit(solution)/shard_map/pool/all_to_all | solution.py:163
  13.8 3.4 %all-to-all-start.1 = ((f32[8,64,128]{2,1,0:T(8,128)}), f32[8,64,128]{2,1,0:T(8,128)S(1)}, u32[]{:S(2)}, u32[]{:S(2)}) async-start(f32[8,64,128]{2,1,0:T(8,128)} %get-tuple-element.8), calls=%async_computation.1 | async-start | bytes 524288 | tf_op jit(solution)/shard_map/pool/all_to_all | solution.py:163
  17.3 3.8 %collective-permute-start = (f32[520,128]{1,0:T(8,128)S(1)}, f32[520,128]{1,0:T(8,128)S(1)}, u32[]{:S(2)}, u32[]{:S(2)}) collective-permute-start(f32[520,128]{1,0:T(8,128)S(1)} %select_maximum_fusion.rest_2_), channel_id=1, source_target_pairs={{0,1},{1,2},{2,3},{3,4},{4,5},{5,6},{6,7},{7,8},{8,9},{9,10},{10,1... | collective-permute-start | bytes 798728 | tf_op jit(solution)/shard_map/pool/ppermute | solution.py:167
  21.1 2.1 %collective-permute-start.1 = (f32[520,128]{1,0:T(8,128)S(1)}, f32[520,128]{1,0:T(8,128)S(1)}, u32[]{:S(2)}, u32[]{:S(2)}) collective-permute-start(f32[520,128]{1,0:T(8,128)S(1)} %select_maximum_fusion.rest_2_), channel_id=1, source_target_pairs={{1,0},{2,1},{3,2},{4,3},{5,4},{6,5},{7,6},{8,7},{9,8},{10,9},{11,1... | collective-permute-start | bytes 798728 | tf_op jit(solution)/shard_map/pool/ppermute | solution.py:168
  23.2 1.5 %all-to-all-done.1 = f32[8,64,128]{2,1,0:T(8,128)S(1)} async-done(((f32[8,64,128]{2,1,0:T(8,128)}), f32[8,64,128]{2,1,0:T(8,128)S(1)}, u32[]{:S(2)}, u32[]{:S(2)}) %all-to-all-start.1) | async-done | bytes 262176 | tf_op jit(solution)/shard_map/pool/all_to_all | solution.py:163
  24.7 4.3 %collective-permute-start.2 = (f32[512,128]{1,0:T(8,128)S(1)}, f32[512,128]{1,0:T(8,128)S(1)}, u32[]{:S(2)}, u32[]{:S(2)}) collective-permute-start(f32[512,128]{1,0:T(8,128)S(1)} %bitcast.13), channel_id=1, source_target_pairs={{0,1},{1,2},{2,3},{3,4},{4,5},{5,6},{6,7},{7,8},{8,9},{9,10},{10,1... | collective-permute-start | bytes 786440 | tf_op jit(solution)/shard_map/pool/ppermute | solution.py:167
  29.0 1.9 %collective-permute-start.3 = (f32[512,128]{1,0:T(8,128)S(1)}, f32[512,128]{1,0:T(8,128)S(1)}, u32[]{:S(2)}, u32[]{:S(2)}) collective-permute-start(f32[512,128]{1,0:T(8,128)S(1)} %bitcast.14), channel_id=1, source_target_pairs={{1,0},{2,1},{3,2},{4,3},{5,4},{6,5},{7,6},{8,7},{9,8},{10,9},{11,1... | collective-permute-start | bytes 786440 | tf_op jit(solution)/shard_map/pool/ppermute | solution.py:168
  31.0 0.0 copy-start
  31.0 1.6 %copy-done = f32[1,1,4,8,128,128]{5,4,3,2,1,0:T(8,128)S(1)} copy-done((f32[1,1,4,8,128,128]{5,4,3,2,1,0:T(8,128)S(1)}, f32[1,1,4,8,128,128]{5,4,3,2,1,0:T(8,128)}, u32[]{:S(2)}) %copy-start) | copy-done | bytes 2097176
  32.6 0.3 split.1.rest_6_
  32.8 1.7 %collective-permute-done.2.rest_1_ = f32[512,128]{1,0:T(8,128)S(1)} collective-permute-done((f32[512,128]{1,0:T(8,128)S(1)}, f32[512,128]{1,0:T(8,128)S(1)}, u32[]{:S(2)}, u32[]{:S(2)}) %collective-permute-start.2) | collective-permute-done | bytes 262176 | tf_op jit(solution)/shard_map/pool/ppermute | solution.py:167
  34.5 6.2 %collective-permute-done.3.rest_5_ = f32[512,128]{1,0:T(8,128)S(1)} collective-permute-done((f32[512,128]{1,0:T(8,128)S(1)}, f32[512,128]{1,0:T(8,128)S(1)}, u32[]{:S(2)}, u32[]{:S(2)}) %collective-permute-start.3) | collective-permute-done | bytes 262176 | tf_op jit(solution)/shard_map/pool/ppermute | solution.py:168
  40.8 0.0 collective-permute-done.rest_0_
  40.8 0.0 collective-permute-done.1.rest_4_
  40.8 0.0 copy-done.1
  40.8 1.3 %remap.1 = f32[4,4,64,128]{3,2,1,0:T(8,128)} custom-call(s32[4,8]{1,0:T(4,128)S(1)} %bitcast.17, f32[520,128]{1,0:T(8,128)S(1)} %collective-permute-done.rest_0_, f32[512,128]{1,0:T(8,128)S(1)} %collective-permute-done.2.rest_1_, f32[520,128]{1,0:T(8,128)S(1)} %select_maximum_fusion.rest_2_, f32[512,128]{1,0:T(8,128)S(1)} %bitcast.15, ...), custom_call_target="tpu_custom_call" | custom-call | flops 268435456 | bytes 4194304 | tf_op jit(solution)/shard_map/remap/remap/pallas_call | solution.py:90
  42.1 10.2 %all-to-all-start.2 = ((f32[4,4,64,128]{3,2,1,0:T(8,128)}), f32[4,4,64,128]{3,2,1,0:T(8,128)S(1)}, u32[]{:S(2)}, u32[]{:S(2)}) async-start(f32[4,4,64,128]{3,2,1,0:T(8,128)} %remap.1), calls=%async_computation.2 | async-start | bytes 1048576 | tf_op jit(solution)/shard_map/halo/all_to_all | solution.py:175
  52.4 6.5 %all-to-all-done.2 = f32[4,4,64,128]{3,2,1,0:T(8,128)S(1)} async-done(((f32[4,4,64,128]{3,2,1,0:T(8,128)}), f32[4,4,64,128]{3,2,1,0:T(8,128)S(1)}, u32[]{:S(2)}, u32[]{:S(2)}) %all-to-all-start.2) | async-done | bytes 524320 | tf_op jit(solution)/shard_map/halo/all_to_all | solution.py:175
  58.8 1.3 %collective-permute-start.4 = (f32[2,4,64,128]{3,2,1,0:T(8,128)S(1)}, f32[2,4,64,128]{3,2,1,0:T(8,128)S(1)}, u32[]{:S(2)}, u32[]{:S(2)}) collective-permute-start(f32[2,4,64,128]{3,2,1,0:T(8,128)S(1)} %constant_dynamic-slice_fusion), channel_id=1, source_target_pairs={{0,4},{1,5},{4,8},{5,9},{6,2},{7,3},{8,12},{9,13},{10,6},{11,7},{1... | collective-permute-start | bytes 786440 | tf_op jit(solution)/shard_map/halo/ppermute | solution.py:182
  60.2 6.9 %collective-permute-done.4 = f32[2,4,64,128]{3,2,1,0:T(8,128)S(1)} collective-permute-done((f32[2,4,64,128]{3,2,1,0:T(8,128)S(1)}, f32[2,4,64,128]{3,2,1,0:T(8,128)S(1)}, u32[]{:S(2)}, u32[]{:S(2)}) %collective-permute-start.4) | collective-permute-done | bytes 262176 | tf_op jit(solution)/shard_map/halo/ppermute | solution.py:182
  67.1 0.9 %smooth.1 = f32[4,64,128]{2,1,0:T(8,128)} custom-call(s32[5,16]{1,0:T(8,128)S(1)} %concatenate.7.index, f32[16,64,128]{2,1,0:T(8,128)S(1)} %bitcast.11, f32[8,64,128]{2,1,0:T(8,128)S(1)} %bitcast.16), custom_call_target="tpu_custom_call" | custom-call | flops 1048576 | bytes 1048576 | tf_op jit(solution)/shard_map/sweeps/smooth/pallas_call | solution.py:131
  (8 shorter events, 0.1 us)
Async XLA Ops:
  1.8 12.0 %all-to-all-start = ((f32[8,64,128]{2,1,0:T(8,128)}), f32[8,64,128]{2,1,0:T(8,128)S(1)}, u32[]{:S(2)}, u32[]{:S(2)}) async-start(f32[8,64,128]{2,1,0:T(8,128)} %get-tuple-element.7), calls=%async_computation | async-start | bytes 524288 | tf_op jit(solution)/shard_map/pool/all_to_all | solution.py:163
  13.8 10.9 %all-to-all-start.1 = ((f32[8,64,128]{2,1,0:T(8,128)}), f32[8,64,128]{2,1,0:T(8,128)S(1)}, u32[]{:S(2)}, u32[]{:S(2)}) async-start(f32[8,64,128]{2,1,0:T(8,128)} %get-tuple-element.8), calls=%async_computation.1 | async-start | bytes 524288 | tf_op jit(solution)/shard_map/pool/all_to_all | solution.py:163
  17.3 23.5 %collective-permute-start = (f32[520,128]{1,0:T(8,128)S(1)}, f32[520,128]{1,0:T(8,128)S(1)}, u32[]{:S(2)}, u32[]{:S(2)}) collective-permute-start(f32[520,128]{1,0:T(8,128)S(1)} %select_maximum_fusion.rest_2_), channel_id=1, source_target_pairs={{0,1},{1,2},{2,3},{3,4},{4,5},{5,6},{6,7},{7,8},{8,9},{9,10},{10,1... | collective-permute-start | bytes 798728 | tf_op jit(solution)/shard_map/pool/ppermute | solution.py:167
  21.1 19.7 %collective-permute-start.1 = (f32[520,128]{1,0:T(8,128)S(1)}, f32[520,128]{1,0:T(8,128)S(1)}, u32[]{:S(2)}, u32[]{:S(2)}) collective-permute-start(f32[520,128]{1,0:T(8,128)S(1)} %select_maximum_fusion.rest_2_), channel_id=1, source_target_pairs={{1,0},{2,1},{3,2},{4,3},{5,4},{6,5},{7,6},{8,7},{9,8},{10,9},{11,1... | collective-permute-start | bytes 798728 | tf_op jit(solution)/shard_map/pool/ppermute | solution.py:168
  24.7 9.8 %collective-permute-start.2 = (f32[512,128]{1,0:T(8,128)S(1)}, f32[512,128]{1,0:T(8,128)S(1)}, u32[]{:S(2)}, u32[]{:S(2)}) collective-permute-start(f32[512,128]{1,0:T(8,128)S(1)} %bitcast.13), channel_id=1, source_target_pairs={{0,1},{1,2},{2,3},{3,4},{4,5},{5,6},{6,7},{7,8},{8,9},{9,10},{10,1... | collective-permute-start | bytes 786440 | tf_op jit(solution)/shard_map/pool/ppermute | solution.py:167
  29.0 11.7 %collective-permute-start.3 = (f32[512,128]{1,0:T(8,128)S(1)}, f32[512,128]{1,0:T(8,128)S(1)}, u32[]{:S(2)}, u32[]{:S(2)}) collective-permute-start(f32[512,128]{1,0:T(8,128)S(1)} %bitcast.14), channel_id=1, source_target_pairs={{1,0},{2,1},{3,2},{4,3},{5,4},{6,5},{7,6},{8,7},{9,8},{10,9},{11,1... | collective-permute-start | bytes 786440 | tf_op jit(solution)/shard_map/pool/ppermute | solution.py:168
  31.0 1.6 %copy-start = (f32[1,1,4,8,128,128]{5,4,3,2,1,0:T(8,128)S(1)}, f32[1,1,4,8,128,128]{5,4,3,2,1,0:T(8,128)}, u32[]{:S(2)}) copy-start(f32[1,1,4,8,128,128]{5,4,3,2,1,0:T(8,128)} %param.8) | copy-start | bytes 6291460
  32.6 8.2 %copy-start.1 = (s32[1,1,4,8]{3,2,1,0:T(4,128)S(1)}, s32[1,1,4,8]{3,2,1,0:T(4,128)}, u32[]{:S(2)}) copy-start(s32[1,1,4,8]{3,2,1,0:T(4,128)} %param.7) | copy-start | bytes 388
  42.1 16.7 %all-to-all-start.2 = ((f32[4,4,64,128]{3,2,1,0:T(8,128)}), f32[4,4,64,128]{3,2,1,0:T(8,128)S(1)}, u32[]{:S(2)}, u32[]{:S(2)}) async-start(f32[4,4,64,128]{3,2,1,0:T(8,128)} %remap.1), calls=%async_computation.2 | async-start | bytes 1048576 | tf_op jit(solution)/shard_map/halo/all_to_all | solution.py:175
  58.8 8.3 %collective-permute-start.4 = (f32[2,4,64,128]{3,2,1,0:T(8,128)S(1)}, f32[2,4,64,128]{3,2,1,0:T(8,128)S(1)}, u32[]{:S(2)}, u32[]{:S(2)}) collective-permute-start(f32[2,4,64,128]{3,2,1,0:T(8,128)S(1)} %constant_dynamic-slice_fusion), channel_id=1, source_target_pairs={{0,4},{1,5},{4,8},{5,9},{6,2},{7,3},{8,12},{9,13},{10,6},{11,7},{1... | collective-permute-start | bytes 786440 | tf_op jit(solution)/shard_map/halo/ppermute | solution.py:182

commit v4 on v2

--- a/solution.py
+++ b/solution.py
@@ -67,8 +67,8 @@
     )(weights)
 
 
-def remap_kernel(slots, source, low, own, high, weights, out, pool):
-    copies, tiles, feat, cells = out.shape
+def remap_kernel(slots, source, low, own, high, weights, out, spread, pool):
+    copies, tiles, feat, cells = spread.shape
     entries = pool.shape[0]
     chosen = source[...]
     for side, part in enumerate((low, own, high)):
@@ -80,8 +80,9 @@
         left = jnp.concatenate(halves(left), axis=0)
         product = jnp.dot(left, weights[b], preferred_element_type=jnp.float32)
         total = product[:feat, :cells] + (product[:feat, cells:] + product[feat:, :cells])
+        out[b] = total
         for copy in range(copies):
-            out[copy, b] = total
+            spread[copy, b] = total
 
 
 def remap(source, low, own, high, weights, groups, slots, feat):
@@ -89,9 +90,12 @@
     cells = width // 2
     return pl.pallas_call(
         functools.partial(remap_kernel, slots),
-        out_shape=jax.ShapeDtypeStruct((QUAD, tiles, feat, cells), jnp.float32),
+        out_shape=[
+            jax.ShapeDtypeStruct((tiles, feat, cells), jnp.float32),
+            jax.ShapeDtypeStruct((QUAD, tiles, feat, cells), jnp.float32),
+        ],
         in_specs=[VMEM] * 5,
-        out_specs=VMEM,
+        out_specs=[VMEM, VMEM],
         scratch_shapes=[pltpu.VMEM((3 * groups * slots, feat, cells), jnp.float32)],
         compiler_params=PARAMS,
         cost_estimate=pl.CostEstimate(flops=8 * tiles * feat * depth * cells, bytes_accessed=2**22, transcendentals=0),
@@ -99,16 +103,20 @@
     )(source, low, own, high, weights)
 
 
-def smooth_kernel(index, quad, halo, out, state, first):
+def smooth_kernel(index, quad, near, far, out, state, first):
     tiles = out.shape[0]
-    edge, middle = halo.shape[0], quad.shape[0]
+    middle = quad.shape[0]
     degree = index.shape[1] // tiles
     spot = index[...]
-    for t in range(edge):
-        state[t] = halo[t]
-        state[edge + middle + t] = halo[t]
+    inner = spot[4, 1] == 1
+    for t in range(tiles):
+        state[t] = far[t]
+        state[3 * tiles + middle + t] = far[t]
+        beside = jnp.where(inner, far[t], near[t])
+        state[tiles + t] = beside
+        state[2 * tiles + middle + t] = beside
     for t in range(middle):
-        state[edge + t] = quad[t]
+        state[2 * tiles + t] = quad[t]
     for e in range(3):
         for b in range(tiles):
             mine = state[spot[4, 0] + (e * tiles + b)]
@@ -124,23 +132,22 @@
         out[b] = mine + 0.15 * (total - 4.0 * mine)
 
 
-def smooth(index, quad, halo):
+def smooth(index, quad, near, far):
     middle, feat, cells = quad.shape
     tiles = middle // QUAD
-    edge = halo.shape[0]
     return pl.pallas_call(
         smooth_kernel,
         out_shape=jax.ShapeDtypeStruct((tiles, feat, cells), jnp.float32),
-        in_specs=[VMEM, VMEM, VMEM],
+        in_specs=[VMEM] * 4,
         out_specs=VMEM,
         scratch_shapes=[
-            pltpu.VMEM((edge + middle + edge, feat, cells), jnp.float32),
+            pltpu.VMEM((middle + 4 * tiles, feat, cells), jnp.float32),
             pltpu.VMEM((3 * tiles, feat, cells), jnp.float32),
         ],
         compiler_params=PARAMS,
         cost_estimate=pl.CostEstimate(flops=2**20, bytes_accessed=2**20, transcendentals=0),
         name="smooth",
-    )(index, quad, halo)
+    )(index, quad, near, far)
 
 
 def shards(atm_blocks, send_list, weight_src, weights, ocean_nbrs):
@@ -165,18 +172,18 @@
         high = lax.ppermute(own, "dev", backward)
 
     with jax.named_scope("remap"):
-        spread = remap(weight_src[0, 0], low, own, high, split(weights[0, 0]), groups, slots, feat)
+        state, spread = remap(weight_src[0, 0], low, own, high, split(weights[0, 0]), groups, slots, feat)
 
     with jax.named_scope("halo"):
+        ends, twos = [], []
+        for start in range(QUAD, count, QUAD):
+            ends += [(start - 1, start), (start, start - 1)]
+            for i in (start - 2, start - 1):
+                twos += [(i, i + 2), (i + 2, i)]
+        near = lax.ppermute(state, "dev", ends)
+        far = lax.ppermute(state, "dev", twos)
         rings = [[z * QUAD + i for i in range(QUAD)] for z in range(count // QUAD)]
         quad = lax.all_to_all(spread, "dev", split_axis=0, concat_axis=0, axis_index_groups=rings, tiled=True)
-        edge = lax.dynamic_slice_in_dim(quad, jnp.where(x < 2, 2, 0), 2, axis=0)
-        hops = []
-        for i in range(count):
-            target = i + QUAD if i % QUAD < 2 else i - QUAD
-            if 0 <= target < count:
-                hops.append((i, target))
-        halo = lax.ppermute(edge, "dev", hops)
 
     with jax.named_scope("sweeps"):
 
@@ -192,11 +199,11 @@
                 mine + (centre - tiles),
                 after + centre,
                 mine,
-                jnp.full((1, tiles * degree), centre - tiles, jnp.int32),
+                jnp.where(jnp.arange(tiles * degree) == 1, (x % 3 != 0).astype(jnp.int32), centre - tiles)[None],
             ],
             axis=0,
         )
-        state = smooth(index, quad.reshape(QUAD * tiles, feat, cells), halo.reshape(2 * tiles, feat, cells))
+        state = smooth(index, quad.reshape(QUAD * tiles, feat, cells), near, far)
     return state[None, None]
 
 

time: 66.6 us -> 65.6 us (0.985)
  the two profiles are of different devices: /device:TPU:6 before, /device:TPU:480 now
where the time goes in v4:
time: 65.6 us; the launch traced here: 65.2 us
  starting transfers between devices  30.6 us (47%)
  waiting for transfers between devices  27.4 us (42%)
  Pallas kernels  5.52 us (8%)
  local copies, waits for them, and re-layouts  0.8 us (1%)
  other arithmetic  0.74 us (1%)
    all_to_all x1, starting transfers between devices, shards(): lax.all_to_all(spread, 'dev', split_axis=0, concat_axis=0, axis_index_gro...  9.79 us
    all_to_all x1, waiting for transfers between devices, shards(): lax.all_to_all(picked, 'grp', split_axis=0, concat_axis=0, tiled=True)  9.58 us
    ppermute x1, waiting for transfers between devices, shards(): low = lax.ppermute(own, 'dev', forward)  9.37 us
    all_to_all x1, waiting for transfers between devices, shards(): lax.all_to_all(spread, 'dev', split_axis=0, concat_axis=0, axis_index_gro...  7.35 us
    ppermute x1, starting transfers between devices, shards(): near = lax.ppermute(state, 'dev', ends)  6.49 us
    ppermute x1, starting transfers between devices, shards(): high = lax.ppermute(own, 'dev', backward)  4.55 us
    all_to_all x1, starting transfers between devices, shards(): lax.all_to_all(picked, 'grp', split_axis=0, concat_axis=0, tiled=True)  4.48 us
    ppermute x1, starting transfers between devices, shards(): low = lax.ppermute(own, 'dev', forward)  3.4 us
  transfers between devices with their start and end apart: 6, of which 4 were waited for; matrix products, arithmetic and copies ran while one was open for 2% of the time, Pallas kernels for 0%

profile of v4, /device:TPU:480, one launch (start us, length us, event | category | flops | bytes accessed | tf_op | source)
XLA Modules:
  0.0 65.2 jit_solution(956395693946418871)
XLA Ops:
  0.0 0.0 copy-start
  0.0 1.9 %pick.1 = f32[8,2,64,128]{3,2,1,0:T(8,128)} custom-call(s32[2,8]{1,0:T(2,128)} %bitcast.14, f32[8,64,128]{2,1,0:T(8,128)} %bitcast.13), custom_call_target="tpu_custom_call" | custom-call | bytes 524288 | tf_op jit(solution)/shard_map/pool/pick/pallas_call | solution.py:30
  1.9 4.5 %all-to-all-start = ((f32[8,2,64,128]{3,2,1,0:T(8,128)}), f32[8,2,64,128]{3,2,1,0:T(8,128)S(1)}, u32[]{:S(2)}, u32[]{:S(2)}) async-start(f32[8,2,64,128]{3,2,1,0:T(8,128)} %pick.1), calls=%async_computation | async-start | bytes 1048576 | tf_op jit(solution)/shard_map/pool/all_to_all | solution.py:165
  6.4 0.8 %squeeze.17 = s32[1,16]{1,0:T(1,128)S(1)} reshape(s32[1,1,4,4]{3,2,1,0:T(4,128)} %param.9) | data formatting | bytes 128 | tf_op jit(solution)/shard_map/squeeze | solution.py:155
  7.2 9.6 %all-to-all-done = f32[8,2,64,128]{3,2,1,0:T(8,128)S(1)} async-done(((f32[8,2,64,128]{3,2,1,0:T(8,128)}), f32[8,2,64,128]{3,2,1,0:T(8,128)S(1)}, u32[]{:S(2)}, u32[]{:S(2)}) %all-to-all-start) | async-done | bytes 524320 | tf_op jit(solution)/shard_map/pool/all_to_all | solution.py:165
  16.8 3.4 %collective-permute-start = (f32[1032,128]{1,0:T(8,128)S(1)}, f32[1032,128]{1,0:T(8,128)}, u32[]{:S(2)}, u32[]{:S(2)}) collective-permute-start(f32[1032,128]{1,0:T(8,128)S(1)} %select_maximum_fusion.own), channel_id=1, source_target_pairs={{0,1},{1,2},{2,3},{3,4},{4,5},{5,6},{6,7},{7,8},{8,9},{9,10},{10,1... | collective-permute-start | bytes 1585160 | tf_op jit(solution)/shard_map/pool/ppermute | solution.py:171
  20.2 4.6 %collective-permute-start.1 = (f32[1032,128]{1,0:T(8,128)S(1)}, f32[1032,128]{1,0:T(8,128)S(1)}, u32[]{:S(2)}, u32[]{:S(2)}) collective-permute-start(f32[1032,128]{1,0:T(8,128)S(1)} %select_maximum_fusion.own), channel_id=1, source_target_pairs={{1,0},{2,1},{3,2},{4,3},{5,4},{6,5},{7,6},{8,7},{9,8},{10,9},{11,1... | collective-permute-start | bytes 1585160 | tf_op jit(solution)/shard_map/pool/ppermute | solution.py:172
  24.8 0.0 copy-done
  24.8 0.0 copy-start.1
  24.8 0.3 split.1.weights
  25.1 9.4 %collective-permute-done.low = f32[1032,128]{1,0:T(8,128)} collective-permute-done((f32[1032,128]{1,0:T(8,128)S(1)}, f32[1032,128]{1,0:T(8,128)}, u32[]{:S(2)}, u32[]{:S(2)}) %collective-permute-start) | collective-permute-done | bytes 528416 | tf_op jit(solution)/shard_map/pool/ppermute | solution.py:171
  34.5 1.1 %collective-permute-done.1.high = f32[1032,128]{1,0:T(8,128)S(1)} collective-permute-done((f32[1032,128]{1,0:T(8,128)S(1)}, f32[1032,128]{1,0:T(8,128)S(1)}, u32[]{:S(2)}, u32[]{:S(2)}) %collective-permute-start.1) | collective-permute-done | bytes 528416 | tf_op jit(solution)/shard_map/pool/ppermute | solution.py:172
  35.6 0.0 copy-done.1
  35.6 2.4 %remap.1 = (f32[4,64,128]{2,1,0:T(8,128)S(1)}, f32[4,4,64,128]{3,2,1,0:T(8,128)}) custom-call(s32[4,8]{1,0:T(4,128)S(1)} %bitcast.11, f32[1032,128]{1,0:T(8,128)} %collective-permute-done.low, f32[1032,128]{1,0:T(8,128)S(1)} %select_maximum_fusion.own, f32[1032,128]{1,0:T(8,128)S(1)} %collective-permute-done.1.high, bf16[4,1024,256]{2,1,0:T(8,128)(2,1)S(1)} %split.1.weights), custom_call_target="tpu_custom_call" | custom-call | flops 268435456 | bytes 4194304 | tf_op jit(solution)/shard_map/remap/remap/pallas_call | solution.py:91
  38.0 6.5 %collective-permute-start.2 = (f32[4,64,128]{2,1,0:T(8,128)S(1)}, f32[4,64,128]{2,1,0:T(8,128)S(1)}, u32[]{:S(2)}, u32[]{:S(2)}) collective-permute-start(f32[4,64,128]{2,1,0:T(8,128)S(1)} %get-tuple-element.8), channel_id=1, source_target_pairs={{3,4},{4,3},{7,8},{8,7},{11,12},{12,11},{15,16},{16,15},{19,20},{2... | collective-permute-start | bytes 393224 | tf_op jit(solution)/shard_map/halo/ppermute | solution.py:183
  44.5 1.9 %collective-permute-start.3 = (f32[4,64,128]{2,1,0:T(8,128)S(1)}, f32[4,64,128]{2,1,0:T(8,128)S(1)}, u32[]{:S(2)}, u32[]{:S(2)}) collective-permute-start(f32[4,64,128]{2,1,0:T(8,128)S(1)} %get-tuple-element.8), channel_id=1, source_target_pairs={{2,4},{4,2},{3,5},{5,3},{6,8},{8,6},{7,9},{9,7},{10,12},{12,10},{1... | collective-permute-start | bytes 393224 | tf_op jit(solution)/shard_map/halo/ppermute | solution.py:184
  46.4 9.8 %all-to-all-start.1 = ((f32[4,4,64,128]{3,2,1,0:T(8,128)}), f32[4,4,64,128]{3,2,1,0:T(8,128)S(1)}, u32[]{:S(2)}, u32[]{:S(2)}) async-start(f32[4,4,64,128]{3,2,1,0:T(8,128)} %get-tuple-element.7), calls=%async_computation.1 | async-start | bytes 1048576 | tf_op jit(solution)/shard_map/halo/all_to_all | solution.py:186
  56.2 0.7 %fusion.1 = s32[1,16]{1,0:T(1,128)S(1)} fusion(f32[1032,128]{1,0:T(8,128)} %collective-permute-done.low, s32[]{:T(128)S(6)} %mul.3), kind=kLoop, calls=%fused_computation.7 | loop fusion | flops 32 | bytes 132 | tf_op jit(solution)/shard_map/sweeps/add | solution.py:198
  56.9 0.0 collective-permute-done.2.near
  56.9 0.0 collective-permute-done.3.far
  56.9 7.4 %all-to-all-done.1 = f32[4,4,64,128]{3,2,1,0:T(8,128)S(1)} async-done(((f32[4,4,64,128]{3,2,1,0:T(8,128)}), f32[4,4,64,128]{3,2,1,0:T(8,128)S(1)}, u32[]{:S(2)}, u32[]{:S(2)}) %all-to-all-start.1) | async-done | bytes 524320 | tf_op jit(solution)/shard_map/halo/all_to_all | solution.py:186
  64.3 0.9 %smooth.1 = f32[4,64,128]{2,1,0:T(8,128)} custom-call(s32[5,16]{1,0:T(8,128)S(1)} %concatenate.7.index, f32[16,64,128]{2,1,0:T(8,128)S(1)} %bitcast.9, f32[4,64,128]{2,1,0:T(8,128)S(1)} %collective-permute-done.2.near, f32[4,64,128]{2,1,0:T(8,128)S(1)} %collective-permute-done.3.far), custom_call_target="tpu_custom_call" | custom-call | flops 1048576 | bytes 1048576 | tf_op jit(solution)/shard_map/sweeps/smooth/pallas_call | solution.py:138
  (5 shorter events, 0.1 us)
Async XLA Ops:
  0.0 24.8 %copy-start = (f32[1,1,4,8,128,128]{5,4,3,2,1,0:T(8,128)S(1)}, f32[1,1,4,8,128,128]{5,4,3,2,1,0:T(8,128)}, u32[]{:S(2)}) copy-start(f32[1,1,4,8,128,128]{5,4,3,2,1,0:T(8,128)} %param.8) | copy-start | bytes 6291460
  1.9 14.8 %all-to-all-start = ((f32[8,2,64,128]{3,2,1,0:T(8,128)}), f32[8,2,64,128]{3,2,1,0:T(8,128)S(1)}, u32[]{:S(2)}, u32[]{:S(2)}) async-start(f32[8,2,64,128]{3,2,1,0:T(8,128)} %pick.1), calls=%async_computation | async-start | bytes 1048576 | tf_op jit(solution)/shard_map/pool/all_to_all | solution.py:165
  16.8 17.7 %collective-permute-start = (f32[1032,128]{1,0:T(8,128)S(1)}, f32[1032,128]{1,0:T(8,128)}, u32[]{:S(2)}, u32[]{:S(2)}) collective-permute-start(f32[1032,128]{1,0:T(8,128)S(1)} %select_maximum_fusion.own), channel_id=1, source_target_pairs={{0,1},{1,2},{2,3},{3,4},{4,5},{5,6},{6,7},{7,8},{8,9},{9,10},{10,1... | collective-permute-start | bytes 1585160 | tf_op jit(solution)/shard_map/pool/ppermute | solution.py:171
  20.2 15.3 %collective-permute-start.1 = (f32[1032,128]{1,0:T(8,128)S(1)}, f32[1032,128]{1,0:T(8,128)S(1)}, u32[]{:S(2)}, u32[]{:S(2)}) collective-permute-start(f32[1032,128]{1,0:T(8,128)S(1)} %select_maximum_fusion.own), channel_id=1, source_target_pairs={{1,0},{2,1},{3,2},{4,3},{5,4},{6,5},{7,6},{8,7},{9,8},{10,9},{11,1... | collective-permute-start | bytes 1585160 | tf_op jit(solution)/shard_map/pool/ppermute | solution.py:172
  24.8 10.7 %copy-start.1 = (s32[1,1,4,8]{3,2,1,0:T(4,128)S(1)}, s32[1,1,4,8]{3,2,1,0:T(4,128)}, u32[]{:S(2)}) copy-start(s32[1,1,4,8]{3,2,1,0:T(4,128)} %param.7) | copy-start | bytes 388
  38.0 18.9 %collective-permute-start.2 = (f32[4,64,128]{2,1,0:T(8,128)S(1)}, f32[4,64,128]{2,1,0:T(8,128)S(1)}, u32[]{:S(2)}, u32[]{:S(2)}) collective-permute-start(f32[4,64,128]{2,1,0:T(8,128)S(1)} %get-tuple-element.8), channel_id=1, source_target_pairs={{3,4},{4,3},{7,8},{8,7},{11,12},{12,11},{15,16},{16,15},{19,20},{2... | collective-permute-start | bytes 393224 | tf_op jit(solution)/shard_map/halo/ppermute | solution.py:183
  44.5 12.4 %collective-permute-start.3 = (f32[4,64,128]{2,1,0:T(8,128)S(1)}, f32[4,64,128]{2,1,0:T(8,128)S(1)}, u32[]{:S(2)}, u32[]{:S(2)}) collective-permute-start(f32[4,64,128]{2,1,0:T(8,128)S(1)} %get-tuple-element.8), channel_id=1, source_target_pairs={{2,4},{4,2},{3,5},{5,3},{6,8},{8,6},{7,9},{9,7},{10,12},{12,10},{1... | collective-permute-start | bytes 393224 | tf_op jit(solution)/shard_map/halo/ppermute | solution.py:184
  46.4 17.9 %all-to-all-start.1 = ((f32[4,4,64,128]{3,2,1,0:T(8,128)}), f32[4,4,64,128]{3,2,1,0:T(8,128)S(1)}, u32[]{:S(2)}, u32[]{:S(2)}) async-start(f32[4,4,64,128]{3,2,1,0:T(8,128)} %get-tuple-element.7), calls=%async_computation.1 | async-start | bytes 1048576 | tf_op jit(solution)/shard_map/halo/all_to_all | solution.py:186

commit v5 on v2

--- a/solution.py
+++ b/solution.py
@@ -67,11 +67,12 @@
     )(weights)
 
 
-def remap_kernel(slots, source, low, own, high, weights, out, pool):
-    copies, tiles, feat, cells = out.shape
+def remap_kernel(slots, source, first, own, second, weights, out, pool):
+    tiles, feat, cells = out.shape
     entries = pool.shape[0]
     chosen = source[...]
-    for side, part in enumerate((low, own, high)):
+    swap = 2 * (1 - lax.rem(lax.axis_index("dev"), 2))
+    for side, part in ((swap, first), (1, own), (2 - swap, second)):
         for entry in range(entries // 3):
             s, c = divmod(entry, slots)
             pool[(s * 3 + side) * slots + c] = part[entry * feat : (entry + 1) * feat, :]
@@ -80,38 +81,40 @@
         left = jnp.concatenate(halves(left), axis=0)
         product = jnp.dot(left, weights[b], preferred_element_type=jnp.float32)
         total = product[:feat, :cells] + (product[:feat, cells:] + product[feat:, :cells])
-        for copy in range(copies):
-            out[copy, b] = total
-
-
-def remap(source, low, own, high, weights, groups, slots, feat):
+        out[b] = total
+
+
+def remap(source, first, own, second, weights, groups, slots, feat):
     tiles, depth, width = weights.shape
     cells = width // 2
     return pl.pallas_call(
         functools.partial(remap_kernel, slots),
-        out_shape=jax.ShapeDtypeStruct((QUAD, tiles, feat, cells), jnp.float32),
+        out_shape=jax.ShapeDtypeStruct((tiles, feat, cells), jnp.float32),
         in_specs=[VMEM] * 5,
         out_specs=VMEM,
         scratch_shapes=[pltpu.VMEM((3 * groups * slots, feat, cells), jnp.float32)],
         compiler_params=PARAMS,
         cost_estimate=pl.CostEstimate(flops=8 * tiles * feat * depth * cells, bytes_accessed=2**22, transcendentals=0),
         name="remap",
-    )(source, low, own, high, weights)
-
-
-def smooth_kernel(index, quad, halo, out, state, first):
+    )(source, first, own, second, weights)
+
+
+def smooth_kernel(index, own, inner, ring, outer, across, out, state, first):
     tiles = out.shape[0]
-    edge, middle = halo.shape[0], quad.shape[0]
     degree = index.shape[1] // tiles
     spot = index[...]
-    for t in range(edge):
-        state[t] = halo[t]
-        state[edge + middle + t] = halo[t]
-    for t in range(middle):
-        state[edge + t] = quad[t]
+    place = lax.axis_index("dev")
+    odd = lax.rem(place, 2) == 1
+    upper = lax.rem(place, QUAD) >= 2
+    for t in range(tiles):
+        state[t] = jnp.where(upper, ring[t], across[t])
+        state[tiles + t] = jnp.where(odd, inner[t], outer[t])
+        state[2 * tiles + t] = own[t]
+        state[3 * tiles + t] = jnp.where(odd, outer[t], inner[t])
+        state[4 * tiles + t] = jnp.where(upper, across[t], ring[t])
     for e in range(3):
         for b in range(tiles):
-            mine = state[spot[4, 0] + (e * tiles + b)]
+            mine = state[(e + 1) * tiles + b]
             total = state[spot[e, b * degree]]
             for m in range(1, degree):
                 total = total + state[spot[e, b * degree + m]]
@@ -124,23 +127,21 @@
         out[b] = mine + 0.15 * (total - 4.0 * mine)
 
 
-def smooth(index, quad, halo):
-    middle, feat, cells = quad.shape
-    tiles = middle // QUAD
-    edge = halo.shape[0]
+def smooth(index, *parts):
+    tiles, feat, cells = parts[0].shape
     return pl.pallas_call(
         smooth_kernel,
         out_shape=jax.ShapeDtypeStruct((tiles, feat, cells), jnp.float32),
-        in_specs=[VMEM, VMEM, VMEM],
+        in_specs=[VMEM] * (1 + len(parts)),
         out_specs=VMEM,
         scratch_shapes=[
-            pltpu.VMEM((edge + middle + edge, feat, cells), jnp.float32),
+            pltpu.VMEM((5 * tiles, feat, cells), jnp.float32),
             pltpu.VMEM((3 * tiles, feat, cells), jnp.float32),
         ],
         compiler_params=PARAMS,
         cost_estimate=pl.CostEstimate(flops=2**20, bytes_accessed=2**20, transcendentals=0),
         name="smooth",
-    )(index, quad, halo)
+    )(index, *parts)
 
 
 def shards(atm_blocks, send_list, weight_src, weights, ocean_nbrs):
@@ -159,44 +160,32 @@
         rows = groups * slots * feat
         listed = jnp.pad(nbrs.astype(jnp.float32).reshape(1, tiles * degree), ((0, 7), (0, cells - tiles * degree)))
         own = jnp.concatenate([arrived.reshape(rows, cells), listed], axis=0)
-        forward = [(i, i + 1) for i in range(count - 1)]
-        backward = [(i + 1, i) for i in range(count - 1)]
-        low = lax.ppermute(own, "dev", forward)
-        high = lax.ppermute(own, "dev", backward)
+        first = lax.ppermute(own, "dev", [(i, i ^ 1) for i in range(count)])
+        second = lax.ppermute(own, "dev", [(i, ((i + 1) ^ 1) - 1) for i in range(1, count - 1)])
+        odd = lax.rem(place, 2) == 1
 
     with jax.named_scope("remap"):
-        spread = remap(weight_src[0, 0], low, own, high, split(weights[0, 0]), groups, slots, feat)
+        first_list = first[rows : rows + 1, : tiles * degree]
+        second_list = second[rows : rows + 1, : tiles * degree]
+        low_list = jnp.where(odd, first_list, second_list)
+        high_list = jnp.where(odd, second_list, first_list)
+        state = remap(weight_src[0, 0], first, own, second, split(pltpu.with_memory_space_constraint(weights[0, 0], pltpu.HBM)), groups, slots, feat)
 
     with jax.named_scope("halo"):
-        rings = [[z * QUAD + i for i in range(QUAD)] for z in range(count // QUAD)]
-        quad = lax.all_to_all(spread, "dev", split_axis=0, concat_axis=0, axis_index_groups=rings, tiled=True)
-        edge = lax.dynamic_slice_in_dim(quad, jnp.where(x < 2, 2, 0), 2, axis=0)
-        hops = []
-        for i in range(count):
-            target = i + QUAD if i % QUAD < 2 else i - QUAD
-            if 0 <= target < count:
-                hops.append((i, target))
-        halo = lax.ppermute(edge, "dev", hops)
+        inner = lax.ppermute(state, "dev", [(i, i ^ 1) for i in range(count)])
+        ring = lax.ppermute(state, "dev", [(i, i ^ 2) for i in range(count)])
+        outer = lax.ppermute(state, "dev", [(i, ((i + 1) ^ 1) - 1) for i in range(1, count - 1)])
+        across = lax.ppermute(state, "dev", [(i, ((i + 2) ^ 2) - 2) for i in range(2, count - 2)])
 
     with jax.named_scope("sweeps"):
 
         def listed_of(payload):
             return payload[rows : rows + 1, : tiles * degree].astype(jnp.int32)
 
-        centre = 2 * tiles + x * tiles
-        after = jnp.where(place == count - 1, 3 * tiles - 1, listed_of(high))
+        after = jnp.where(place == count - 1, 3 * tiles - 1, high_list.astype(jnp.int32))
         mine = nbrs.reshape(1, tiles * degree)
-        index = jnp.concatenate(
-            [
-                listed_of(low) + (centre - 2 * tiles),
-                mine + (centre - tiles),
-                after + centre,
-                mine,
-                jnp.full((1, tiles * degree), centre - tiles, jnp.int32),
-            ],
-            axis=0,
-        )
-        state = smooth(index, quad.reshape(QUAD * tiles, feat, cells), halo.reshape(2 * tiles, feat, cells))
+        index = jnp.concatenate([low_list.astype(jnp.int32), mine + tiles, after + 2 * tiles, mine], axis=0)
+        state = smooth(index, state, inner, ring, outer, across)
     return state[None, None]
 
 

time: 66.6 us -> 61.8 us (0.928)
  the two profiles are of different devices: /device:TPU:6 before, /device:TPU:8 now
where the time goes in v5:
time: 61.8 us; the launch traced here: 61.4 us
  starting transfers between devices  27.9 us (45%)
  waiting for transfers between devices  27.5 us (44%)
  Pallas kernels  5.1 us (8%)
  local copies, waits for them, and re-layouts  0.77 us (1%)
    all_to_all x1, starting transfers between devices, shards(): lax.all_to_all(picked, 'grp', split_axis=0, concat_axis=0, tiled=True)  16.5 us
    ppermute x1, waiting for transfers between devices, shards(): first = lax.ppermute(own, 'dev', [(i, i ^ 1) for i in range(count)])  14.4 us
    all_to_all x1, waiting for transfers between devices, shards(): lax.all_to_all(picked, 'grp', split_axis=0, concat_axis=0, tiled=True)  8.15 us
    ppermute x1, starting transfers between devices, shards(): ring = lax.ppermute(state, 'dev', [(i, i ^ 2) for i in range(count)])  5.51 us
    ppermute x1, waiting for transfers between devices, shards(): inner = lax.ppermute(state, 'dev', [(i, i ^ 1) for i in range(count)])  2.84 us
    ppermute x1, waiting for transfers between devices, shards(): ring = lax.ppermute(state, 'dev', [(i, i ^ 2) for i in range(count)])  2.02 us
    ppermute x1, starting transfers between devices, shards(): inner = lax.ppermute(state, 'dev', [(i, i ^ 1) for i in range(count)])  1.92 us
    ppermute x1, starting transfers between devices, shards(): first = lax.ppermute(own, 'dev', [(i, i ^ 1) for i in range(count)])  1.92 us
  transfers between devices with their start and end apart: 7, of which 4 were waited for; matrix products, arithmetic and copies ran while one was open for 1% of the time, Pallas kernels for 3%

profile of v5, /device:TPU:8, one launch (start us, length us, event | category | flops | bytes accessed | tf_op | source)
XLA Modules:
  0.0 61.4 jit_solution(2328805456825342894)
XLA Ops:
  0.0 1.8 %pick.1 = f32[8,2,64,128]{3,2,1,0:T(8,128)} custom-call(s32[2,8]{1,0:T(2,128)} %bitcast.12, f32[8,64,128]{2,1,0:T(8,128)} %bitcast.11), custom_call_target="tpu_custom_call" | custom-call | bytes 524288 | tf_op jit(solution)/shard_map/pool/pick/pallas_call | solution.py:30
  1.8 16.5 %all-to-all-start = ((f32[8,2,64,128]{3,2,1,0:T(8,128)}), f32[8,2,64,128]{3,2,1,0:T(8,128)S(1)}, u32[]{:S(2)}, u32[]{:S(2)}) async-start(f32[8,2,64,128]{3,2,1,0:T(8,128)} %pick.1), calls=%async_computation | async-start | bytes 1048576 | tf_op jit(solution)/shard_map/pool/all_to_all | solution.py:159
  18.3 0.8 %squeeze.17 = s32[1,16]{1,0:T(1,128)S(1)} reshape(s32[1,1,4,4]{3,2,1,0:T(4,128)} %param.9) | data formatting | bytes 128 | tf_op jit(solution)/shard_map/squeeze | solution.py:149
  19.1 8.1 %all-to-all-done = f32[8,2,64,128]{3,2,1,0:T(8,128)S(1)} async-done(((f32[8,2,64,128]{3,2,1,0:T(8,128)}), f32[8,2,64,128]{3,2,1,0:T(8,128)S(1)}, u32[]{:S(2)}, u32[]{:S(2)}) %all-to-all-start) | async-done | bytes 524320 | tf_op jit(solution)/shard_map/pool/all_to_all | solution.py:159
  27.3 0.7 %collective-permute-start.1 = (f32[1032,128]{1,0:T(8,128)S(1)}, f32[1032,128]{1,0:T(8,128)S(1)}, u32[]{:S(2)}, u32[]{:S(2)}) collective-permute-start(f32[1032,128]{1,0:T(8,128)S(1)} %select_maximum_fusion.own), channel_id=1, source_target_pairs={{1,2},{2,1},{3,4},{4,3},{5,6},{6,5},{7,8},{8,7},{9,10},{10,9},{11,... | collective-permute-start | bytes 1585160 | tf_op jit(solution)/shard_map/pool/ppermute | solution.py:164
  28.0 1.9 %collective-permute-start = (f32[1032,128]{1,0:T(8,128)S(1)}, f32[1032,128]{1,0:T(8,128)S(1)}, u32[]{:S(2)}, u32[]{:S(2)}) collective-permute-start(f32[1032,128]{1,0:T(8,128)S(1)} %select_maximum_fusion.own), channel_id=1, source_target_pairs={{0,1},{1,0},{2,3},{3,2},{4,5},{5,4},{6,7},{7,6},{8,9},{9,8},{10,11... | collective-permute-start | bytes 1585160 | tf_op jit(solution)/shard_map/pool/ppermute | solution.py:163
  29.9 0.0 copy-start
  29.9 1.9 %split.1.weights = bf16[4,1024,256]{2,1,0:T(8,128)(2,1)S(1)} custom-call(f32[4,8,128,128]{3,2,1,0:T(8,128)} %bitcast.9), custom_call_target="tpu_custom_call" | custom-call | flops 1048576 | bytes 4194304 | tf_op jit(solution)/shard_map/remap/split/pallas_call | solution.py:59
  31.8 0.0 collective-permute-done.1.second
  31.8 14.4 %collective-permute-done.first = f32[1032,128]{1,0:T(8,128)S(1)} collective-permute-done((f32[1032,128]{1,0:T(8,128)S(1)}, f32[1032,128]{1,0:T(8,128)S(1)}, u32[]{:S(2)}, u32[]{:S(2)}) %collective-permute-start) | collective-permute-done | bytes 528416 | tf_op jit(solution)/shard_map/pool/ppermute | solution.py:163
  46.2 0.0 copy-done
  46.2 0.5 remap.1.own
  46.8 0.7 %collective-permute-start.5 = (f32[4,64,128]{2,1,0:T(8,128)S(1)}, f32[4,64,128]{2,1,0:T(8,128)S(1)}, u32[]{:S(2)}, u32[]{:S(2)}) collective-permute-start(f32[4,64,128]{2,1,0:T(8,128)S(1)} %remap.1.own), channel_id=1, source_target_pairs={{2,4},{3,5},{4,2},{5,3},{6,8},{7,9},{8,6},{9,7},{10,12},{11,13},{1... | collective-permute-start | bytes 393224 | tf_op jit(solution)/shard_map/halo/ppermute | solution.py:178
  47.5 0.7 %collective-permute-start.4 = (f32[4,64,128]{2,1,0:T(8,128)S(1)}, f32[4,64,128]{2,1,0:T(8,128)S(1)}, u32[]{:S(2)}, u32[]{:S(2)}) collective-permute-start(f32[4,64,128]{2,1,0:T(8,128)S(1)} %remap.1.own), channel_id=1, source_target_pairs={{1,2},{2,1},{3,4},{4,3},{5,6},{6,5},{7,8},{8,7},{9,10},{10,9},{11,... | collective-permute-start | bytes 393224 | tf_op jit(solution)/shard_map/halo/ppermute | solution.py:177
  48.1 5.5 %collective-permute-start.3 = (f32[4,64,128]{2,1,0:T(8,128)S(1)}, f32[4,64,128]{2,1,0:T(8,128)S(1)}, u32[]{:S(2)}, u32[]{:S(2)}) collective-permute-start(f32[4,64,128]{2,1,0:T(8,128)S(1)} %remap.1.own), channel_id=1, source_target_pairs={{0,2},{1,3},{2,0},{3,1},{4,6},{5,7},{6,4},{7,5},{8,10},{9,11},{10,... | collective-permute-start | bytes 393224 | tf_op jit(solution)/shard_map/halo/ppermute | solution.py:176
  53.7 1.9 %collective-permute-start.2 = (f32[4,64,128]{2,1,0:T(8,128)S(1)}, f32[4,64,128]{2,1,0:T(8,128)S(1)}, u32[]{:S(2)}, u32[]{:S(2)}) collective-permute-start(f32[4,64,128]{2,1,0:T(8,128)S(1)} %remap.1.own), channel_id=1, source_target_pairs={{0,1},{1,0},{2,3},{3,2},{4,5},{5,4},{6,7},{7,6},{8,9},{9,8},{10,11... | collective-permute-start | bytes 393224 | tf_op jit(solution)/shard_map/halo/ppermute | solution.py:175
  55.6 0.0 collective-permute-done.5.across
  55.7 0.0 collective-permute-done.4.outer
  55.7 2.0 %collective-permute-done.3.ring = f32[4,64,128]{2,1,0:T(8,128)S(1)} collective-permute-done((f32[4,64,128]{2,1,0:T(8,128)S(1)}, f32[4,64,128]{2,1,0:T(8,128)S(1)}, u32[]{:S(2)}, u32[]{:S(2)}) %collective-permute-start.3) | collective-permute-done | bytes 131104 | tf_op jit(solution)/shard_map/halo/ppermute | solution.py:176
  57.7 2.8 %collective-permute-done.2.inner = f32[4,64,128]{2,1,0:T(8,128)S(1)} collective-permute-done((f32[4,64,128]{2,1,0:T(8,128)S(1)}, f32[4,64,128]{2,1,0:T(8,128)S(1)}, u32[]{:S(2)}, u32[]{:S(2)}) %collective-permute-start.2) | collective-permute-done | bytes 131104 | tf_op jit(solution)/shard_map/halo/ppermute | solution.py:175
  60.5 0.9 %smooth.1 = f32[4,64,128]{2,1,0:T(8,128)} custom-call(s32[4,16]{1,0:T(4,128)S(1)} %pad_add_fusion.index, f32[4,64,128]{2,1,0:T(8,128)S(1)} %remap.1.own, f32[4,64,128]{2,1,0:T(8,128)S(1)} %collective-permute-done.2.inner, f32[4,64,128]{2,1,0:T(8,128)S(1)} %collective-permute-done.3.ring, f32[4,64,128]{2,1,0:T(8,128)S(1)} %collective-permute-done.4.outer, ...), custom_call_target="tpu_custom_call" | custom-call | flops 1048576 | bytes 1048576 | tf_op jit(solution)/shard_map/sweeps/smooth/pallas_call | solution.py:132
  (5 shorter events, 0.1 us)
Async XLA Ops:
  1.8 25.4 %all-to-all-start = ((f32[8,2,64,128]{3,2,1,0:T(8,128)}), f32[8,2,64,128]{3,2,1,0:T(8,128)S(1)}, u32[]{:S(2)}, u32[]{:S(2)}) async-start(f32[8,2,64,128]{3,2,1,0:T(8,128)} %pick.1), calls=%async_computation | async-start | bytes 1048576 | tf_op jit(solution)/shard_map/pool/all_to_all | solution.py:159
  27.3 4.5 %collective-permute-start.1 = (f32[1032,128]{1,0:T(8,128)S(1)}, f32[1032,128]{1,0:T(8,128)S(1)}, u32[]{:S(2)}, u32[]{:S(2)}) collective-permute-start(f32[1032,128]{1,0:T(8,128)S(1)} %select_maximum_fusion.own), channel_id=1, source_target_pairs={{1,2},{2,1},{3,4},{4,3},{5,6},{6,5},{7,8},{8,7},{9,10},{10,9},{11,... | collective-permute-start | bytes 1585160 | tf_op jit(solution)/shard_map/pool/ppermute | solution.py:164
  28.0 18.3 %collective-permute-start = (f32[1032,128]{1,0:T(8,128)S(1)}, f32[1032,128]{1,0:T(8,128)S(1)}, u32[]{:S(2)}, u32[]{:S(2)}) collective-permute-start(f32[1032,128]{1,0:T(8,128)S(1)} %select_maximum_fusion.own), channel_id=1, source_target_pairs={{0,1},{1,0},{2,3},{3,2},{4,5},{5,4},{6,7},{7,6},{8,9},{9,8},{10,11... | collective-permute-start | bytes 1585160 | tf_op jit(solution)/shard_map/pool/ppermute | solution.py:163
  29.9 16.3 %copy-start = (s32[1,1,4,8]{3,2,1,0:T(4,128)S(1)}, s32[1,1,4,8]{3,2,1,0:T(4,128)}, u32[]{:S(2)}) copy-start(s32[1,1,4,8]{3,2,1,0:T(4,128)} %param.7) | copy-start | bytes 388
  46.8 8.9 %collective-permute-start.5 = (f32[4,64,128]{2,1,0:T(8,128)S(1)}, f32[4,64,128]{2,1,0:T(8,128)S(1)}, u32[]{:S(2)}, u32[]{:S(2)}) collective-permute-start(f32[4,64,128]{2,1,0:T(8,128)S(1)} %remap.1.own), channel_id=1, source_target_pairs={{2,4},{3,5},{4,2},{5,3},{6,8},{7,9},{8,6},{9,7},{10,12},{11,13},{1... | collective-permute-start | bytes 393224 | tf_op jit(solution)/shard_map/halo/ppermute | solution.py:178
  47.5 8.2 %collective-permute-start.4 = (f32[4,64,128]{2,1,0:T(8,128)S(1)}, f32[4,64,128]{2,1,0:T(8,128)S(1)}, u32[]{:S(2)}, u32[]{:S(2)}) collective-permute-start(f32[4,64,128]{2,1,0:T(8,128)S(1)} %remap.1.own), channel_id=1, source_target_pairs={{1,2},{2,1},{3,4},{4,3},{5,6},{6,5},{7,8},{8,7},{9,10},{10,9},{11,... | collective-permute-start | bytes 393224 | tf_op jit(solution)/shard_map/halo/ppermute | solution.py:177
  48.1 9.5 %collective-permute-start.3 = (f32[4,64,128]{2,1,0:T(8,128)S(1)}, f32[4,64,128]{2,1,0:T(8,128)S(1)}, u32[]{:S(2)}, u32[]{:S(2)}) collective-permute-start(f32[4,64,128]{2,1,0:T(8,128)S(1)} %remap.1.own), channel_id=1, source_target_pairs={{0,2},{1,3},{2,0},{3,1},{4,6},{5,7},{6,4},{7,5},{8,10},{9,11},{10,... | collective-permute-start | bytes 393224 | tf_op jit(solution)/shard_map/halo/ppermute | solution.py:176
  53.7 6.9 %collective-permute-start.2 = (f32[4,64,128]{2,1,0:T(8,128)S(1)}, f32[4,64,128]{2,1,0:T(8,128)S(1)}, u32[]{:S(2)}, u32[]{:S(2)}) collective-permute-start(f32[4,64,128]{2,1,0:T(8,128)S(1)} %remap.1.own), channel_id=1, source_target_pairs={{0,1},{1,0},{2,3},{3,2},{4,5},{5,4},{6,7},{7,6},{8,9},{9,8},{10,11... | collective-permute-start | bytes 393224 | tf_op jit(solution)/shard_map/halo/ppermute | solution.py:175

commit v6 on v5

--- a/solution.py
+++ b/solution.py
@@ -13,34 +13,49 @@
 PARAMS = pltpu.CompilerParams(vmem_limit_bytes=24 * 1024 * 1024)
 
 
-def pick_kernel(lists, atm, out, chosen, blocks, sems):
+def pick_kernel(lists, nbrs, atm, out, listed, chosen, beside, blocks, sems):
     first = pltpu.make_async_copy(lists, chosen, sems.at[0])
-    second = pltpu.make_async_copy(atm, blocks, sems.at[1])
+    second = pltpu.make_async_copy(nbrs, beside, sems.at[1])
+    third = pltpu.make_async_copy(atm, blocks, sems.at[2])
     first.start()
     second.start()
+    third.start()
     first.wait()
     second.wait()
+    lane = lax.broadcasted_iota(jnp.int32, listed.shape, 1)
+    row = jnp.zeros(listed.shape, jnp.int32)
+    tiles, degree = beside.shape
+    for b in range(tiles):
+        for m in range(degree):
+            row = jnp.where(lane == b * degree + m, beside[b, m], row)
+    listed[...] = row.astype(jnp.float32)
+    third.wait()
     for g in range(out.shape[0]):
         for c in range(out.shape[1]):
             out[g, c] = blocks[chosen[c, g]]
 
 
-def pick(lists, atm):
+def pick(lists, nbrs, atm):
     slots, groups = lists.shape
+    inputs = (pltpu.with_memory_space_constraint(a, pltpu.HBM) for a in (lists, nbrs, atm))
     return pl.pallas_call(
         pick_kernel,
-        out_shape=jax.ShapeDtypeStruct((groups, slots) + atm.shape[1:], jnp.float32),
-        in_specs=[HBM, HBM],
-        out_specs=VMEM,
+        out_shape=[
+            jax.ShapeDtypeStruct((groups, slots) + atm.shape[1:], jnp.float32),
+            jax.ShapeDtypeStruct((8, atm.shape[2]), jnp.float32),
+        ],
+        in_specs=[HBM, HBM, HBM],
+        out_specs=[VMEM, VMEM],
         scratch_shapes=[
             pltpu.SMEM(lists.shape, jnp.int32),
+            pltpu.SMEM(nbrs.shape, jnp.int32),
             pltpu.VMEM(atm.shape, jnp.float32),
-            pltpu.SemaphoreType.DMA((2,)),
+            pltpu.SemaphoreType.DMA((3,)),
         ],
         compiler_params=PARAMS,
         cost_estimate=pl.CostEstimate(flops=0, bytes_accessed=2**19, transcendentals=0),
         name="pick",
-    )(pltpu.with_memory_space_constraint(lists, pltpu.HBM), pltpu.with_memory_space_constraint(atm, pltpu.HBM))
+    )(*inputs)
 
 
 def halves(x):
@@ -99,13 +114,16 @@
     )(source, first, own, second, weights)
 
 
-def smooth_kernel(index, own, inner, ring, outer, across, out, state, first):
+def smooth_kernel(index, own, inner, ring, across, outer, out, state, first):
     tiles = out.shape[0]
     degree = index.shape[1] // tiles
-    spot = index[...]
+    pair, other, mine = (index[row : row + 1, :] for row in range(3))
     place = lax.axis_index("dev")
     odd = lax.rem(place, 2) == 1
     upper = lax.rem(place, QUAD) >= 2
+    after = jnp.where(odd, other, pair)
+    after = jnp.where(place == lax.axis_size("dev") - 1, 3 * tiles - 1, after)
+    lists = (jnp.where(odd, pair, other), mine, after)
     for t in range(tiles):
         state[t] = jnp.where(upper, ring[t], across[t])
         state[tiles + t] = jnp.where(odd, inner[t], outer[t])
@@ -114,17 +132,17 @@
         state[4 * tiles + t] = jnp.where(upper, across[t], ring[t])
     for e in range(3):
         for b in range(tiles):
-            mine = state[(e + 1) * tiles + b]
-            total = state[spot[e, b * degree]]
+            here = state[(e + 1) * tiles + b]
+            total = state[e * tiles + lists[e][0, b * degree]]
             for m in range(1, degree):
-                total = total + state[spot[e, b * degree + m]]
-            first[e * tiles + b] = mine + 0.15 * (total - 4.0 * mine)
-    for b in range(tiles):
-        mine = first[tiles + b]
-        total = first[spot[3, b * degree]]
+                total = total + state[e * tiles + lists[e][0, b * degree + m]]
+            first[e * tiles + b] = here + 0.15 * (total - 4.0 * here)
+    for b in range(tiles):
+        here = first[tiles + b]
+        total = first[mine[0, b * degree]]
         for m in range(1, degree):
-            total = total + first[spot[3, b * degree + m]]
-        out[b] = mine + 0.15 * (total - 4.0 * mine)
+            total = total + first[mine[0, b * degree + m]]
+        out[b] = here + 0.15 * (total - 4.0 * here)
 
 
 def smooth(index, *parts):
@@ -151,24 +169,16 @@
     feat, cells = atm_blocks.shape[3:]
     tiles, degree = nbrs.shape
     count = lax.axis_size("dev")
-    place = lax.axis_index("dev")
-    x = lax.rem(place, QUAD)
 
     with jax.named_scope("pool"):
-        picked = pick(lists.T, atm_blocks[0, 0])
+        picked, listed = pick(lists.T, nbrs, atm_blocks[0, 0])
         arrived = lax.all_to_all(picked, "grp", split_axis=0, concat_axis=0, tiled=True)
+        arrived, listed = lax.optimization_barrier((arrived, listed))
         rows = groups * slots * feat
-        listed = jnp.pad(nbrs.astype(jnp.float32).reshape(1, tiles * degree), ((0, 7), (0, cells - tiles * degree)))
         own = jnp.concatenate([arrived.reshape(rows, cells), listed], axis=0)
         first = lax.ppermute(own, "dev", [(i, i ^ 1) for i in range(count)])
         second = lax.ppermute(own, "dev", [(i, ((i + 1) ^ 1) - 1) for i in range(1, count - 1)])
-        odd = lax.rem(place, 2) == 1
-
-    with jax.named_scope("remap"):
-        first_list = first[rows : rows + 1, : tiles * degree]
-        second_list = second[rows : rows + 1, : tiles * degree]
-        low_list = jnp.where(odd, first_list, second_list)
-        high_list = jnp.where(odd, second_list, first_list)
+        listed = [part[rows : rows + 1, : tiles * degree] for part in (first, second, own)]
         state = remap(weight_src[0, 0], first, own, second, split(pltpu.with_memory_space_constraint(weights[0, 0], pltpu.HBM)), groups, slots, feat)
 
     with jax.named_scope("halo"):
@@ -182,10 +192,8 @@
         def listed_of(payload):
             return payload[rows : rows + 1, : tiles * degree].astype(jnp.int32)
 
-        after = jnp.where(place == count - 1, 3 * tiles - 1, high_list.astype(jnp.int32))
-        mine = nbrs.reshape(1, tiles * degree)
-        index = jnp.concatenate([low_list.astype(jnp.int32), mine + tiles, after + 2 * tiles, mine], axis=0)
-        state = smooth(index, state, inner, ring, outer, across)
+        index = jnp.concatenate(listed, axis=0).astype(jnp.int32)
+        state = smooth(index, state, inner, ring, across, outer)
     return state[None, None]
 
 

time: 61.8 us -> 59.5 us (0.963)
  the two profiles are of different devices: /device:TPU:8 before, /device:TPU:2 now
where the time goes in v6:
time: 59.5 us; the launch traced here: 59.1 us
  starting transfers between devices  25.7 us (43%)
  blocking collectives  14.7 us (25%)
  waiting for transfers between devices  14.3 us (24%)
  Pallas kernels  4.33 us (7%)
    all_to_all x1, blocking collectives, shards(): lax.all_to_all(picked, 'grp', split_axis=0, concat_axis=0, tiled=True)  14.7 us
    ppermute x1, starting transfers between devices, shards(): first = lax.ppermute(own, 'dev', [(i, i ^ 1) for i in range(count)])  10.5 us
    ppermute x1, waiting for transfers between devices, shards(): first = lax.ppermute(own, 'dev', [(i, i ^ 1) for i in range(count)])  9.75 us
    ppermute x1, starting transfers between devices, shards(): inner = lax.ppermute(state, 'dev', [(i, i ^ 1) for i in range(count)])  7 us
    ppermute x1, waiting for transfers between devices, shards(): inner = lax.ppermute(state, 'dev', [(i, i ^ 1) for i in range(count)])  4.52 us
    ppermute x1, starting transfers between devices, shards(): lax.ppermute(own, 'dev', [(i, (i + 1 ^ 1) - 1) for i in range(1, count -...  3.4 us
    ppermute x1, starting transfers between devices, shards(): ring = lax.ppermute(state, 'dev', [(i, i ^ 2) for i in range(count)])  2.15 us
    ppermute x1, starting transfers between devices, shards(): lax.ppermute(state, 'dev', [(i, (i + 1 ^ 1) - 1) for i in range(1, count...  1.92 us
  transfers between devices with their start and end apart: 6, of which 2 were waited for; matrix products, arithmetic and copies ran while one was open for 0% of the time, Pallas kernels for 3%

profile of v6, /device:TPU:2, one launch (start us, length us, event | category | flops | bytes accessed | tf_op | source)
XLA Modules:
  0.0 59.1 jit_solution(17840331651726080172)
XLA Ops:
  0.0 1.0 %pick.1 = (f32[8,2,64,128]{3,2,1,0:T(8,128)S(1)}, f32[8,128]{1,0:T(8,128)S(1)}) custom-call(s32[2,8]{1,0:T(2,128)} %bitcast.14, s32[4,4]{1,0:T(4,128)} %bitcast.13, f32[8,64,128]{2,1,0:T(8,128)} %bitcast.12), custom_call_target="tpu_custom_call" | custom-call | bytes 524288 | tf_op jit(solution)/shard_map/pool/pick/pallas_call | solution.py:41
  1.0 14.7 %all_to_all.5 = f32[8,2,64,128]{3,2,1,0:T(8,128)S(1)} all-to-all(f32[8,2,64,128]{3,2,1,0:T(8,128)S(1)} %get-tuple-element.9), channel_id=1, replica_groups=mesh['grp'=8,'dev'=128] {'grp'}, dimensions={0} | all-to-all | bytes 1048576 | tf_op jit(solution)/shard_map/pool/all_to_all | solution.py:175
  15.7 3.4 %collective-permute-start.1 = (f32[1032,128]{1,0:T(8,128)S(1)}, f32[1032,128]{1,0:T(8,128)S(1)}, u32[]{:S(2)}, u32[]{:S(2)}) collective-permute-start(f32[1032,128]{1,0:T(8,128)S(1)} %pad_maximum_fusion.own), channel_id=1, source_target_pairs={{1,2},{2,1},{3,4},{4,3},{5,6},{6,5},{7,8},{8,7},{9,10},{10,9},{11,... | collective-permute-start | bytes 1585160 | tf_op jit(solution)/shard_map/pool/ppermute | solution.py:180
  19.1 10.5 %collective-permute-start = (f32[1032,128]{1,0:T(8,128)S(1)}, f32[1032,128]{1,0:T(8,128)S(1)}, u32[]{:S(2)}, u32[]{:S(2)}) collective-permute-start(f32[1032,128]{1,0:T(8,128)S(1)} %pad_maximum_fusion.own), channel_id=1, source_target_pairs={{0,1},{1,0},{2,3},{3,2},{4,5},{5,4},{6,7},{7,6},{8,9},{9,8},{10,11... | collective-permute-start | bytes 1585160 | tf_op jit(solution)/shard_map/pool/ppermute | solution.py:179
  29.7 0.0 copy-start
  29.7 1.9 %split.1.weights = bf16[4,1024,256]{2,1,0:T(8,128)(2,1)S(1)} custom-call(f32[4,8,128,128]{3,2,1,0:T(8,128)} %bitcast.10), custom_call_target="tpu_custom_call" | custom-call | flops 1048576 | bytes 4194304 | tf_op jit(solution)/shard_map/pool/split/pallas_call | solution.py:74
  31.5 0.0 collective-permute-done.1.second
  31.5 9.8 %collective-permute-done.first = f32[1032,128]{1,0:T(8,128)S(1)} collective-permute-done((f32[1032,128]{1,0:T(8,128)S(1)}, f32[1032,128]{1,0:T(8,128)S(1)}, u32[]{:S(2)}, u32[]{:S(2)}) %collective-permute-start) | collective-permute-done | bytes 528416 | tf_op jit(solution)/shard_map/pool/ppermute | solution.py:179
  41.3 0.0 copy-done
  41.3 0.6 remap.1.own
  41.9 1.9 %collective-permute-start.5 = (f32[4,64,128]{2,1,0:T(8,128)S(1)}, f32[4,64,128]{2,1,0:T(8,128)S(1)}, u32[]{:S(2)}, u32[]{:S(2)}) collective-permute-start(f32[4,64,128]{2,1,0:T(8,128)S(1)} %remap.1.own), channel_id=1, source_target_pairs={{1,2},{2,1},{3,4},{4,3},{5,6},{6,5},{7,8},{8,7},{9,10},{10,9},{11,... | collective-permute-start | bytes 393224 | tf_op jit(solution)/shard_map/halo/ppermute | solution.py:187
  43.8 0.7 %collective-permute-start.4 = (f32[4,64,128]{2,1,0:T(8,128)S(1)}, f32[4,64,128]{2,1,0:T(8,128)S(1)}, u32[]{:S(2)}, u32[]{:S(2)}) collective-permute-start(f32[4,64,128]{2,1,0:T(8,128)S(1)} %remap.1.own), channel_id=1, source_target_pairs={{2,4},{3,5},{4,2},{5,3},{6,8},{7,9},{8,6},{9,7},{10,12},{11,13},{1... | collective-permute-start | bytes 393224 | tf_op jit(solution)/shard_map/halo/ppermute | solution.py:188
  44.5 2.1 %collective-permute-start.3 = (f32[4,64,128]{2,1,0:T(8,128)S(1)}, f32[4,64,128]{2,1,0:T(8,128)S(1)}, u32[]{:S(2)}, u32[]{:S(2)}) collective-permute-start(f32[4,64,128]{2,1,0:T(8,128)S(1)} %remap.1.own), channel_id=1, source_target_pairs={{0,2},{1,3},{2,0},{3,1},{4,6},{5,7},{6,4},{7,5},{8,10},{9,11},{10,... | collective-permute-start | bytes 393224 | tf_op jit(solution)/shard_map/halo/ppermute | solution.py:186
  46.6 7.0 %collective-permute-start.2 = (f32[4,64,128]{2,1,0:T(8,128)S(1)}, f32[4,64,128]{2,1,0:T(8,128)S(1)}, u32[]{:S(2)}, u32[]{:S(2)}) collective-permute-start(f32[4,64,128]{2,1,0:T(8,128)S(1)} %remap.1.own), channel_id=1, source_target_pairs={{0,1},{1,0},{2,3},{3,2},{4,5},{5,4},{6,7},{7,6},{8,9},{9,8},{10,11... | collective-permute-start | bytes 393224 | tf_op jit(solution)/shard_map/halo/ppermute | solution.py:185
  53.7 0.0 collective-permute-done.5.outer
  53.7 0.0 collective-permute-done.4.across
  53.7 0.0 collective-permute-done.3.ring
  53.7 4.5 %collective-permute-done.2.inner = f32[4,64,128]{2,1,0:T(8,128)S(1)} collective-permute-done((f32[4,64,128]{2,1,0:T(8,128)S(1)}, f32[4,64,128]{2,1,0:T(8,128)S(1)}, u32[]{:S(2)}, u32[]{:S(2)}) %collective-permute-start.2) | collective-permute-done | bytes 131104 | tf_op jit(solution)/shard_map/halo/ppermute | solution.py:185
  58.2 0.9 %smooth.1 = f32[4,64,128]{2,1,0:T(8,128)} custom-call(s32[3,16]{1,0:T(4,128)S(1)} %maximum_convert_fusion.index, f32[4,64,128]{2,1,0:T(8,128)S(1)} %remap.1.own, f32[4,64,128]{2,1,0:T(8,128)S(1)} %collective-permute-done.2.inner, f32[4,64,128]{2,1,0:T(8,128)S(1)} %collective-permute-done.3.ring, f32[4,64,128]{2,1,0:T(8,128)S(1)} %collective-permute-done.4.across, ...), custom_call_target="tpu_custom_call" | custom-call | flops 1048576 | bytes 1048576 | tf_op jit(solution)/shard_map/sweeps/smooth/pallas_call | solution.py:150
  (5 shorter events, 0.1 us)
Async XLA Ops:
  15.7 15.8 %collective-permute-start.1 = (f32[1032,128]{1,0:T(8,128)S(1)}, f32[1032,128]{1,0:T(8,128)S(1)}, u32[]{:S(2)}, u32[]{:S(2)}) collective-permute-start(f32[1032,128]{1,0:T(8,128)S(1)} %pad_maximum_fusion.own), channel_id=1, source_target_pairs={{1,2},{2,1},{3,4},{4,3},{5,6},{6,5},{7,8},{8,7},{9,10},{10,9},{11,... | collective-permute-start | bytes 1585160 | tf_op jit(solution)/shard_map/pool/ppermute | solution.py:180
  19.1 22.2 %collective-permute-start = (f32[1032,128]{1,0:T(8,128)S(1)}, f32[1032,128]{1,0:T(8,128)S(1)}, u32[]{:S(2)}, u32[]{:S(2)}) collective-permute-start(f32[1032,128]{1,0:T(8,128)S(1)} %pad_maximum_fusion.own), channel_id=1, source_target_pairs={{0,1},{1,0},{2,3},{3,2},{4,5},{5,4},{6,7},{7,6},{8,9},{9,8},{10,11... | collective-permute-start | bytes 1585160 | tf_op jit(solution)/shard_map/pool/ppermute | solution.py:179
  29.7 11.6 %copy-start = (s32[1,1,4,8]{3,2,1,0:T(4,128)S(1)}, s32[1,1,4,8]{3,2,1,0:T(4,128)}, u32[]{:S(2)}) copy-start(s32[1,1,4,8]{3,2,1,0:T(4,128)} %param.7) | copy-start | bytes 388
  41.9 11.8 %collective-permute-start.5 = (f32[4,64,128]{2,1,0:T(8,128)S(1)}, f32[4,64,128]{2,1,0:T(8,128)S(1)}, u32[]{:S(2)}, u32[]{:S(2)}) collective-permute-start(f32[4,64,128]{2,1,0:T(8,128)S(1)} %remap.1.own), channel_id=1, source_target_pairs={{1,2},{2,1},{3,4},{4,3},{5,6},{6,5},{7,8},{8,7},{9,10},{10,9},{11,... | collective-permute-start | bytes 393224 | tf_op jit(solution)/shard_map/halo/ppermute | solution.py:187
  43.8 9.9 %collective-permute-start.4 = (f32[4,64,128]{2,1,0:T(8,128)S(1)}, f32[4,64,128]{2,1,0:T(8,128)S(1)}, u32[]{:S(2)}, u32[]{:S(2)}) collective-permute-start(f32[4,64,128]{2,1,0:T(8,128)S(1)} %remap.1.own), channel_id=1, source_target_pairs={{2,4},{3,5},{4,2},{5,3},{6,8},{7,9},{8,6},{9,7},{10,12},{11,13},{1... | collective-permute-start | bytes 393224 | tf_op jit(solution)/shard_map/halo/ppermute | solution.py:188
  44.5 9.2 %collective-permute-start.3 = (f32[4,64,128]{2,1,0:T(8,128)S(1)}, f32[4,64,128]{2,1,0:T(8,128)S(1)}, u32[]{:S(2)}, u32[]{:S(2)}) collective-permute-start(f32[4,64,128]{2,1,0:T(8,128)S(1)} %remap.1.own), channel_id=1, source_target_pairs={{0,2},{1,3},{2,0},{3,1},{4,6},{5,7},{6,4},{7,5},{8,10},{9,11},{10,... | collective-permute-start | bytes 393224 | tf_op jit(solution)/shard_map/halo/ppermute | solution.py:186
  46.6 11.6 %collective-permute-start.2 = (f32[4,64,128]{2,1,0:T(8,128)S(1)}, f32[4,64,128]{2,1,0:T(8,128)S(1)}, u32[]{:S(2)}, u32[]{:S(2)}) collective-permute-start(f32[4,64,128]{2,1,0:T(8,128)S(1)} %remap.1.own), channel_id=1, source_target_pairs={{0,1},{1,0},{2,3},{3,2},{4,5},{5,4},{6,7},{7,6},{8,9},{9,8},{10,11... | collective-permute-start | bytes 393224 | tf_op jit(solution)/shard_map/halo/ppermute | solution.py:185

commit v7 on v6

--- a/solution.py
+++ b/solution.py
@@ -8,6 +8,7 @@
 from jax.sharding import PartitionSpec as P
 
 QUAD = 4
+DEGREE = 4
 VMEM = pl.BlockSpec(memory_space=pltpu.VMEM)
 HBM = pl.BlockSpec(memory_space=pltpu.HBM)
 PARAMS = pltpu.CompilerParams(vmem_limit_bytes=24 * 1024 * 1024)
@@ -82,7 +83,7 @@
     )(weights)
 
 
-def remap_kernel(slots, source, first, own, second, weights, out, pool):
+def remap_kernel(slots, source, first, own, second, weights, out, lists, pool):
     tiles, feat, cells = out.shape
     entries = pool.shape[0]
     chosen = source[...]
@@ -91,6 +92,8 @@
         for entry in range(entries // 3):
             s, c = divmod(entry, slots)
             pool[(s * 3 + side) * slots + c] = part[entry * feat : (entry + 1) * feat, :]
+    for row, part in enumerate((first, second, own)):
+        lists[row] = part[entries // 3 * feat :, :].astype(jnp.int32)
     for b in range(tiles):
         left = jnp.concatenate([pool[chosen[b, k]] for k in range(source.shape[1])], axis=1)
         left = jnp.concatenate(halves(left), axis=0)
@@ -104,9 +107,12 @@
     cells = width // 2
     return pl.pallas_call(
         functools.partial(remap_kernel, slots),
-        out_shape=jax.ShapeDtypeStruct((tiles, feat, cells), jnp.float32),
+        out_shape=[
+            jax.ShapeDtypeStruct((tiles, feat, cells), jnp.float32),
+            jax.ShapeDtypeStruct((3, first.shape[0] - groups * slots * feat, cells), jnp.int32),
+        ],
         in_specs=[VMEM] * 5,
-        out_specs=VMEM,
+        out_specs=[VMEM, VMEM],
         scratch_shapes=[pltpu.VMEM((3 * groups * slots, feat, cells), jnp.float32)],
         compiler_params=PARAMS,
         cost_estimate=pl.CostEstimate(flops=8 * tiles * feat * depth * cells, bytes_accessed=2**22, transcendentals=0),
@@ -116,8 +122,8 @@
 
 def smooth_kernel(index, own, inner, ring, across, outer, out, state, first):
     tiles = out.shape[0]
-    degree = index.shape[1] // tiles
-    pair, other, mine = (index[row : row + 1, :] for row in range(3))
+    degree = DEGREE
+    pair, other, mine = (index[row, :1, :] for row in range(3))
     place = lax.axis_index("dev")
     odd = lax.rem(place, 2) == 1
     upper = lax.rem(place, QUAD) >= 2
@@ -178,8 +184,7 @@
         own = jnp.concatenate([arrived.reshape(rows, cells), listed], axis=0)
         first = lax.ppermute(own, "dev", [(i, i ^ 1) for i in range(count)])
         second = lax.ppermute(own, "dev", [(i, ((i + 1) ^ 1) - 1) for i in range(1, count - 1)])
-        listed = [part[rows : rows + 1, : tiles * degree] for part in (first, second, own)]
-        state = remap(weight_src[0, 0], first, own, second, split(pltpu.with_memory_space_constraint(weights[0, 0], pltpu.HBM)), groups, slots, feat)
+        state, lists = remap(weight_src[0, 0], first, own, second, split(pltpu.with_memory_space_constraint(weights[0, 0], pltpu.HBM)), groups, slots, feat)
 
     with jax.named_scope("halo"):
         inner = lax.ppermute(state, "dev", [(i, i ^ 1) for i in range(count)])
@@ -192,8 +197,7 @@
         def listed_of(payload):
             return payload[rows : rows + 1, : tiles * degree].astype(jnp.int32)
 
-        index = jnp.concatenate(listed, axis=0).astype(jnp.int32)
-        state = smooth(index, state, inner, ring, across, outer)
+        state = smooth(lists, state, inner, ring, across, outer)
     return state[None, None]
 
 

time: 59.5 us -> 59.5 us (level)
  no operation moved by 1% of the time
where the time goes in v7:
time: 59.5 us; the launch traced here: 59.1 us
  starting transfers between devices  25.7 us (43%)
  blocking collectives  14.7 us (25%)
  waiting for transfers between devices  14.3 us (24%)
  Pallas kernels  4.32 us (7%)
    all_to_all x1, blocking collectives, shards(): lax.all_to_all(picked, 'grp', split_axis=0, concat_axis=0, tiled=True)  14.7 us
    ppermute x1, starting transfers between devices, shards(): first = lax.ppermute(own, 'dev', [(i, i ^ 1) for i in range(count)])  10.5 us
    ppermute x1, waiting for transfers between devices, shards(): first = lax.ppermute(own, 'dev', [(i, i ^ 1) for i in range(count)])  9.75 us
    ppermute x1, starting transfers between devices, shards(): inner = lax.ppermute(state, 'dev', [(i, i ^ 1) for i in range(count)])  7 us
    ppermute x1, waiting for transfers between devices, shards(): inner = lax.ppermute(state, 'dev', [(i, i ^ 1) for i in range(count)])  4.58 us
    ppermute x1, starting transfers between devices, shards(): lax.ppermute(own, 'dev', [(i, (i + 1 ^ 1) - 1) for i in range(1, count -...  3.4 us
    ppermute x1, starting transfers between devices, shards(): ring = lax.ppermute(state, 'dev', [(i, i ^ 2) for i in range(count)])  2.15 us
    ppermute x1, starting transfers between devices, shards(): lax.ppermute(state, 'dev', [(i, (i + 1 ^ 1) - 1) for i in range(1, count...  1.92 us
  transfers between devices with their start and end apart: 6, of which 2 were waited for; matrix products, arithmetic and copies ran while one was open for 0% of the time, Pallas kernels for 3%

profile of v7, /device:TPU:2, one launch (start us, length us, event | category | flops | bytes accessed | tf_op | source)
XLA Modules:
  0.0 59.1 jit_solution(12469689518425036987)
XLA Ops:
  0.0 1.0 %pick.1 = (f32[8,2,64,128]{3,2,1,0:T(8,128)S(1)}, f32[8,128]{1,0:T(8,128)S(1)}) custom-call(s32[2,8]{1,0:T(2,128)} %bitcast.14, s32[4,4]{1,0:T(4,128)} %bitcast.13, f32[8,64,128]{2,1,0:T(8,128)} %bitcast.12), custom_call_target="tpu_custom_call" | custom-call | bytes 524288 | tf_op jit(solution)/shard_map/pool/pick/pallas_call | solution.py:42
  1.0 14.7 %all_to_all.5 = f32[8,2,64,128]{3,2,1,0:T(8,128)S(1)} all-to-all(f32[8,2,64,128]{3,2,1,0:T(8,128)S(1)} %get-tuple-element.11), channel_id=1, replica_groups=mesh['grp'=8,'dev'=128] {'grp'}, dimensions={0} | all-to-all | bytes 1048576 | tf_op jit(solution)/shard_map/pool/all_to_all | solution.py:181
  15.7 3.4 %collective-permute-start.1 = (f32[1032,128]{1,0:T(8,128)S(1)}, f32[1032,128]{1,0:T(8,128)S(1)}, u32[]{:S(2)}, u32[]{:S(2)}) collective-permute-start(f32[1032,128]{1,0:T(8,128)S(1)} %pad_maximum_fusion.own), channel_id=1, source_target_pairs={{1,2},{2,1},{3,4},{4,3},{5,6},{6,5},{7,8},{8,7},{9,10},{10,9},{11,... | collective-permute-start | bytes 1585160 | tf_op jit(solution)/shard_map/pool/ppermute | solution.py:186
  19.1 10.5 %collective-permute-start = (f32[1032,128]{1,0:T(8,128)S(1)}, f32[1032,128]{1,0:T(8,128)S(1)}, u32[]{:S(2)}, u32[]{:S(2)}) collective-permute-start(f32[1032,128]{1,0:T(8,128)S(1)} %pad_maximum_fusion.own), channel_id=1, source_target_pairs={{0,1},{1,0},{2,3},{3,2},{4,5},{5,4},{6,7},{7,6},{8,9},{9,8},{10,11... | collective-permute-start | bytes 1585160 | tf_op jit(solution)/shard_map/pool/ppermute | solution.py:185
  29.7 0.0 copy-start
  29.7 1.9 %split.1.weights = bf16[4,1024,256]{2,1,0:T(8,128)(2,1)S(1)} custom-call(f32[4,8,128,128]{3,2,1,0:T(8,128)} %bitcast.10), custom_call_target="tpu_custom_call" | custom-call | flops 1048576 | bytes 4194304 | tf_op jit(solution)/shard_map/pool/split/pallas_call | solution.py:75
  31.5 0.0 collective-permute-done.1.second
  31.5 9.8 %collective-permute-done.first = f32[1032,128]{1,0:T(8,128)S(1)} collective-permute-done((f32[1032,128]{1,0:T(8,128)S(1)}, f32[1032,128]{1,0:T(8,128)S(1)}, u32[]{:S(2)}, u32[]{:S(2)}) %collective-permute-start) | collective-permute-done | bytes 528416 | tf_op jit(solution)/shard_map/pool/ppermute | solution.py:185
  41.3 0.0 copy-done
  41.3 0.5 remap.1
  41.9 1.9 %collective-permute-start.5 = (f32[4,64,128]{2,1,0:T(8,128)S(1)}, f32[4,64,128]{2,1,0:T(8,128)S(1)}, u32[]{:S(2)}, u32[]{:S(2)}) collective-permute-start(f32[4,64,128]{2,1,0:T(8,128)S(1)} %get-tuple-element.16.own), channel_id=1, source_target_pairs={{1,2},{2,1},{3,4},{4,3},{5,6},{6,5},{7,8},{8,7},{9,10},{10,9},{11,... | collective-permute-start | bytes 393224 | tf_op jit(solution)/shard_map/halo/ppermute | solution.py:192
  43.8 0.7 %collective-permute-start.4 = (f32[4,64,128]{2,1,0:T(8,128)S(1)}, f32[4,64,128]{2,1,0:T(8,128)S(1)}, u32[]{:S(2)}, u32[]{:S(2)}) collective-permute-start(f32[4,64,128]{2,1,0:T(8,128)S(1)} %get-tuple-element.16.own), channel_id=1, source_target_pairs={{2,4},{3,5},{4,2},{5,3},{6,8},{7,9},{8,6},{9,7},{10,12},{11,13},{1... | collective-permute-start | bytes 393224 | tf_op jit(solution)/shard_map/halo/ppermute | solution.py:193
  44.5 2.1 %collective-permute-start.3 = (f32[4,64,128]{2,1,0:T(8,128)S(1)}, f32[4,64,128]{2,1,0:T(8,128)S(1)}, u32[]{:S(2)}, u32[]{:S(2)}) collective-permute-start(f32[4,64,128]{2,1,0:T(8,128)S(1)} %get-tuple-element.16.own), channel_id=1, source_target_pairs={{0,2},{1,3},{2,0},{3,1},{4,6},{5,7},{6,4},{7,5},{8,10},{9,11},{10,... | collective-permute-start | bytes 393224 | tf_op jit(solution)/shard_map/halo/ppermute | solution.py:191
  46.6 7.0 %collective-permute-start.2 = (f32[4,64,128]{2,1,0:T(8,128)S(1)}, f32[4,64,128]{2,1,0:T(8,128)S(1)}, u32[]{:S(2)}, u32[]{:S(2)}) collective-permute-start(f32[4,64,128]{2,1,0:T(8,128)S(1)} %get-tuple-element.16.own), channel_id=1, source_target_pairs={{0,1},{1,0},{2,3},{3,2},{4,5},{5,4},{6,7},{7,6},{8,9},{9,8},{10,11... | collective-permute-start | bytes 393224 | tf_op jit(solution)/shard_map/halo/ppermute | solution.py:190
  53.6 0.0 collective-permute-done.5.outer
  53.6 0.0 collective-permute-done.4.across
  53.6 0.0 collective-permute-done.3.ring
  53.7 4.6 %collective-permute-done.2.inner = f32[4,64,128]{2,1,0:T(8,128)S(1)} collective-permute-done((f32[4,64,128]{2,1,0:T(8,128)S(1)}, f32[4,64,128]{2,1,0:T(8,128)S(1)}, u32[]{:S(2)}, u32[]{:S(2)}) %collective-permute-start.2) | collective-permute-done | bytes 131104 | tf_op jit(solution)/shard_map/halo/ppermute | solution.py:190
  58.2 0.9 %smooth.1 = f32[4,64,128]{2,1,0:T(8,128)} custom-call(s32[3,8,128]{2,1,0:T(8,128)S(1)} %get-tuple-element.15.index, f32[4,64,128]{2,1,0:T(8,128)S(1)} %get-tuple-element.16.own, f32[4,64,128]{2,1,0:T(8,128)S(1)} %collective-permute-done.2.inner, f32[4,64,128]{2,1,0:T(8,128)S(1)} %collective-permute-done.3.ring, ...), custom_call_target="tpu_custom_call" | custom-call | flops 1048576 | bytes 1048576 | tf_op jit(solution)/shard_map/sweeps/smooth/pallas_call | solution.py:156
  (1 shorter events, 0.0 us)
Async XLA Ops:
  15.7 15.8 %collective-permute-start.1 = (f32[1032,128]{1,0:T(8,128)S(1)}, f32[1032,128]{1,0:T(8,128)S(1)}, u32[]{:S(2)}, u32[]{:S(2)}) collective-permute-start(f32[1032,128]{1,0:T(8,128)S(1)} %pad_maximum_fusion.own), channel_id=1, source_target_pairs={{1,2},{2,1},{3,4},{4,3},{5,6},{6,5},{7,8},{8,7},{9,10},{10,9},{11,... | collective-permute-start | bytes 1585160 | tf_op jit(solution)/shard_map/pool/ppermute | solution.py:186
  19.1 22.2 %collective-permute-start = (f32[1032,128]{1,0:T(8,128)S(1)}, f32[1032,128]{1,0:T(8,128)S(1)}, u32[]{:S(2)}, u32[]{:S(2)}) collective-permute-start(f32[1032,128]{1,0:T(8,128)S(1)} %pad_maximum_fusion.own), channel_id=1, source_target_pairs={{0,1},{1,0},{2,3},{3,2},{4,5},{5,4},{6,7},{7,6},{8,9},{9,8},{10,11... | collective-permute-start | bytes 1585160 | tf_op jit(solution)/shard_map/pool/ppermute | solution.py:185
  29.7 11.6 %copy-start = (s32[1,1,4,8]{3,2,1,0:T(4,128)S(1)}, s32[1,1,4,8]{3,2,1,0:T(4,128)}, u32[]{:S(2)}) copy-start(s32[1,1,4,8]{3,2,1,0:T(4,128)} %param.7) | copy-start | bytes 388
  41.9 11.8 %collective-permute-start.5 = (f32[4,64,128]{2,1,0:T(8,128)S(1)}, f32[4,64,128]{2,1,0:T(8,128)S(1)}, u32[]{:S(2)}, u32[]{:S(2)}) collective-permute-start(f32[4,64,128]{2,1,0:T(8,128)S(1)} %get-tuple-element.16.own), channel_id=1, source_target_pairs={{1,2},{2,1},{3,4},{4,3},{5,6},{6,5},{7,8},{8,7},{9,10},{10,9},{11,... | collective-permute-start | bytes 393224 | tf_op jit(solution)/shard_map/halo/ppermute | solution.py:192
  43.8 9.9 %collective-permute-start.4 = (f32[4,64,128]{2,1,0:T(8,128)S(1)}, f32[4,64,128]{2,1,0:T(8,128)S(1)}, u32[]{:S(2)}, u32[]{:S(2)}) collective-permute-start(f32[4,64,128]{2,1,0:T(8,128)S(1)} %get-tuple-element.16.own), channel_id=1, source_target_pairs={{2,4},{3,5},{4,2},{5,3},{6,8},{7,9},{8,6},{9,7},{10,12},{11,13},{1... | collective-permute-start | bytes 393224 | tf_op jit(solution)/shard_map/halo/ppermute | solution.py:193
  44.5 9.2 %collective-permute-start.3 = (f32[4,64,128]{2,1,0:T(8,128)S(1)}, f32[4,64,128]{2,1,0:T(8,128)S(1)}, u32[]{:S(2)}, u32[]{:S(2)}) collective-permute-start(f32[4,64,128]{2,1,0:T(8,128)S(1)} %get-tuple-element.16.own), channel_id=1, source_target_pairs={{0,2},{1,3},{2,0},{3,1},{4,6},{5,7},{6,4},{7,5},{8,10},{9,11},{10,... | collective-permute-start | bytes 393224 | tf_op jit(solution)/shard_map/halo/ppermute | solution.py:191
  46.6 11.6 %collective-permute-start.2 = (f32[4,64,128]{2,1,0:T(8,128)S(1)}, f32[4,64,128]{2,1,0:T(8,128)S(1)}, u32[]{:S(2)}, u32[]{:S(2)}) collective-permute-start(f32[4,64,128]{2,1,0:T(8,128)S(1)} %get-tuple-element.16.own), channel_id=1, source_target_pairs={{0,1},{1,0},{2,3},{3,2},{4,5},{5,4},{6,7},{7,6},{8,9},{9,8},{10,11... | collective-permute-start | bytes 393224 | tf_op jit(solution)/shard_map/halo/ppermute | solution.py:190

commit v8 on v7

--- a/solution.py
+++ b/solution.py
@@ -120,7 +120,7 @@
     )(source, first, own, second, weights)
 
 
-def smooth_kernel(index, own, inner, ring, across, outer, out, state, first):
+def smooth_kernel(index, own, inner, ring, outer, across, out, state, first):
     tiles = out.shape[0]
     degree = DEGREE
     pair, other, mine = (index[row, :1, :] for row in range(3))
@@ -197,7 +197,7 @@
         def listed_of(payload):
             return payload[rows : rows + 1, : tiles * degree].astype(jnp.int32)
 
-        state = smooth(lists, state, inner, ring, across, outer)
+        state = smooth(lists, state, inner, ring, outer, across)
     return state[None, None]
 
 

time: 59.5 us -> 59.8 us (level)
  the two profiles are of different devices: /device:TPU:2 before, /device:TPU:8 now
where the time goes in v8:
time: 59.8 us; the launch traced here: 59.5 us
  blocking collectives  24.4 us (41%)
  waiting for transfers between devices  19.2 us (32%)
  starting transfers between devices  11.4 us (19%)
  Pallas kernels  4.33 us (7%)
    all_to_all x1, blocking collectives, shards(): lax.all_to_all(picked, 'grp', split_axis=0, concat_axis=0, tiled=True)  24.4 us
    ppermute x1, waiting for transfers between devices, shards(): first = lax.ppermute(own, 'dev', [(i, i ^ 1) for i in range(count)])  14.3 us
    ppermute x1, starting transfers between devices, shards(): ring = lax.ppermute(state, 'dev', [(i, i ^ 2) for i in range(count)])  5.5 us
    ppermute x1, waiting for transfers between devices, shards(): inner = lax.ppermute(state, 'dev', [(i, i ^ 1) for i in range(count)])  3.53 us
    ppermute x1, starting transfers between devices, shards(): first = lax.ppermute(own, 'dev', [(i, i ^ 1) for i in range(count)])  1.92 us
    ppermute x1, starting transfers between devices, shards(): inner = lax.ppermute(state, 'dev', [(i, i ^ 1) for i in range(count)])  1.92 us
    pallas_call x1, Pallas kernels, split(): pl.pallas_call(split_kernel, out_shape=jax.ShapeDtypeStruct((tiles, block...  1.85 us
    ppermute x1, waiting for transfers between devices, shards(): ring = lax.ppermute(state, 'dev', [(i, i ^ 2) for i in range(count)])  1.38 us
  transfers between devices with their start and end apart: 6, of which 3 were waited for; matrix products, arithmetic and copies ran while one was open for 0% of the time, Pallas kernels for 3%

profile of v8, /device:TPU:8, one launch (start us, length us, event | category | flops | bytes accessed | tf_op | source)
XLA Modules:
  0.0 59.5 jit_solution(9415366029695304658)
XLA Ops:
  0.0 1.0 %pick.1 = (f32[8,2,64,128]{3,2,1,0:T(8,128)S(1)}, f32[8,128]{1,0:T(8,128)S(1)}) custom-call(s32[2,8]{1,0:T(2,128)} %bitcast.14, s32[4,4]{1,0:T(4,128)} %bitcast.13, f32[8,64,128]{2,1,0:T(8,128)} %bitcast.12), custom_call_target="tpu_custom_call" | custom-call | bytes 524288 | tf_op jit(solution)/shard_map/pool/pick/pallas_call | solution.py:42
  1.0 24.4 %all_to_all.5 = f32[8,2,64,128]{3,2,1,0:T(8,128)S(1)} all-to-all(f32[8,2,64,128]{3,2,1,0:T(8,128)S(1)} %get-tuple-element.11), channel_id=1, replica_groups=mesh['grp'=8,'dev'=128] {'grp'}, dimensions={0} | all-to-all | bytes 1048576 | tf_op jit(solution)/shard_map/pool/all_to_all | solution.py:181
  25.5 0.7 %collective-permute-start.1 = (f32[1032,128]{1,0:T(8,128)S(1)}, f32[1032,128]{1,0:T(8,128)S(1)}, u32[]{:S(2)}, u32[]{:S(2)}) collective-permute-start(f32[1032,128]{1,0:T(8,128)S(1)} %pad_maximum_fusion.own), channel_id=1, source_target_pairs={{1,2},{2,1},{3,4},{4,3},{5,6},{6,5},{7,8},{8,7},{9,10},{10,9},{11,... | collective-permute-start | bytes 1585160 | tf_op jit(solution)/shard_map/pool/ppermute | solution.py:186
  26.2 1.9 %collective-permute-start = (f32[1032,128]{1,0:T(8,128)S(1)}, f32[1032,128]{1,0:T(8,128)S(1)}, u32[]{:S(2)}, u32[]{:S(2)}) collective-permute-start(f32[1032,128]{1,0:T(8,128)S(1)} %pad_maximum_fusion.own), channel_id=1, source_target_pairs={{0,1},{1,0},{2,3},{3,2},{4,5},{5,4},{6,7},{7,6},{8,9},{9,8},{10,11... | collective-permute-start | bytes 1585160 | tf_op jit(solution)/shard_map/pool/ppermute | solution.py:185
  28.1 0.0 copy-start
  28.1 1.9 %split.1.weights = bf16[4,1024,256]{2,1,0:T(8,128)(2,1)S(1)} custom-call(f32[4,8,128,128]{3,2,1,0:T(8,128)} %bitcast.10), custom_call_target="tpu_custom_call" | custom-call | flops 1048576 | bytes 4194304 | tf_op jit(solution)/shard_map/pool/split/pallas_call | solution.py:75
  30.0 0.0 collective-permute-done.1.second
  30.0 14.3 %collective-permute-done.first = f32[1032,128]{1,0:T(8,128)S(1)} collective-permute-done((f32[1032,128]{1,0:T(8,128)S(1)}, f32[1032,128]{1,0:T(8,128)S(1)}, u32[]{:S(2)}, u32[]{:S(2)}) %collective-permute-start) | collective-permute-done | bytes 528416 | tf_op jit(solution)/shard_map/pool/ppermute | solution.py:185
  44.3 0.0 copy-done
  44.3 0.5 remap.1
  44.9 0.7 %collective-permute-start.5 = (f32[4,64,128]{2,1,0:T(8,128)S(1)}, f32[4,64,128]{2,1,0:T(8,128)S(1)}, u32[]{:S(2)}, u32[]{:S(2)}) collective-permute-start(f32[4,64,128]{2,1,0:T(8,128)S(1)} %get-tuple-element.16.own), channel_id=1, source_target_pairs={{2,4},{3,5},{4,2},{5,3},{6,8},{7,9},{8,6},{9,7},{10,12},{11,13},{1... | collective-permute-start | bytes 393224 | tf_op jit(solution)/shard_map/halo/ppermute | solution.py:193
  45.5 0.7 %collective-permute-start.4 = (f32[4,64,128]{2,1,0:T(8,128)S(1)}, f32[4,64,128]{2,1,0:T(8,128)S(1)}, u32[]{:S(2)}, u32[]{:S(2)}) collective-permute-start(f32[4,64,128]{2,1,0:T(8,128)S(1)} %get-tuple-element.16.own), channel_id=1, source_target_pairs={{1,2},{2,1},{3,4},{4,3},{5,6},{6,5},{7,8},{8,7},{9,10},{10,9},{11,... | collective-permute-start | bytes 393224 | tf_op jit(solution)/shard_map/halo/ppermute | solution.py:192
  46.2 5.5 %collective-permute-start.3 = (f32[4,64,128]{2,1,0:T(8,128)S(1)}, f32[4,64,128]{2,1,0:T(8,128)S(1)}, u32[]{:S(2)}, u32[]{:S(2)}) collective-permute-start(f32[4,64,128]{2,1,0:T(8,128)S(1)} %get-tuple-element.16.own), channel_id=1, source_target_pairs={{0,2},{1,3},{2,0},{3,1},{4,6},{5,7},{6,4},{7,5},{8,10},{9,11},{10,... | collective-permute-start | bytes 393224 | tf_op jit(solution)/shard_map/halo/ppermute | solution.py:191
  51.7 1.9 %collective-permute-start.2 = (f32[4,64,128]{2,1,0:T(8,128)S(1)}, f32[4,64,128]{2,1,0:T(8,128)S(1)}, u32[]{:S(2)}, u32[]{:S(2)}) collective-permute-start(f32[4,64,128]{2,1,0:T(8,128)S(1)} %get-tuple-element.16.own), channel_id=1, source_target_pairs={{0,1},{1,0},{2,3},{3,2},{4,5},{5,4},{6,7},{7,6},{8,9},{9,8},{10,11... | collective-permute-start | bytes 393224 | tf_op jit(solution)/shard_map/halo/ppermute | solution.py:190
  53.6 0.0 collective-permute-done.5.across
  53.7 0.0 collective-permute-done.4.outer
  53.7 1.4 %collective-permute-done.3.ring = f32[4,64,128]{2,1,0:T(8,128)S(1)} collective-permute-done((f32[4,64,128]{2,1,0:T(8,128)S(1)}, f32[4,64,128]{2,1,0:T(8,128)S(1)}, u32[]{:S(2)}, u32[]{:S(2)}) %collective-permute-start.3) | collective-permute-done | bytes 131104 | tf_op jit(solution)/shard_map/halo/ppermute | solution.py:191
  55.0 3.5 %collective-permute-done.2.inner = f32[4,64,128]{2,1,0:T(8,128)S(1)} collective-permute-done((f32[4,64,128]{2,1,0:T(8,128)S(1)}, f32[4,64,128]{2,1,0:T(8,128)S(1)}, u32[]{:S(2)}, u32[]{:S(2)}) %collective-permute-start.2) | collective-permute-done | bytes 131104 | tf_op jit(solution)/shard_map/halo/ppermute | solution.py:190
  58.6 0.9 %smooth.1 = f32[4,64,128]{2,1,0:T(8,128)} custom-call(s32[3,8,128]{2,1,0:T(8,128)S(1)} %get-tuple-element.15.index, f32[4,64,128]{2,1,0:T(8,128)S(1)} %get-tuple-element.16.own, f32[4,64,128]{2,1,0:T(8,128)S(1)} %collective-permute-done.2.inner, f32[4,64,128]{2,1,0:T(8,128)S(1)} %collective-permute-done.3.ring, ...), custom_call_target="tpu_custom_call" | custom-call | flops 1048576 | bytes 1048576 | tf_op jit(solution)/shard_map/sweeps/smooth/pallas_call | solution.py:156
  (1 shorter events, 0.0 us)
Async XLA Ops:
  25.5 4.5 %collective-permute-start.1 = (f32[1032,128]{1,0:T(8,128)S(1)}, f32[1032,128]{1,0:T(8,128)S(1)}, u32[]{:S(2)}, u32[]{:S(2)}) collective-permute-start(f32[1032,128]{1,0:T(8,128)S(1)} %pad_maximum_fusion.own), channel_id=1, source_target_pairs={{1,2},{2,1},{3,4},{4,3},{5,6},{6,5},{7,8},{8,7},{9,10},{10,9},{11,... | collective-permute-start | bytes 1585160 | tf_op jit(solution)/shard_map/pool/ppermute | solution.py:186
  26.2 18.1 %collective-permute-start = (f32[1032,128]{1,0:T(8,128)S(1)}, f32[1032,128]{1,0:T(8,128)S(1)}, u32[]{:S(2)}, u32[]{:S(2)}) collective-permute-start(f32[1032,128]{1,0:T(8,128)S(1)} %pad_maximum_fusion.own), channel_id=1, source_target_pairs={{0,1},{1,0},{2,3},{3,2},{4,5},{5,4},{6,7},{7,6},{8,9},{9,8},{10,11... | collective-permute-start | bytes 1585160 | tf_op jit(solution)/shard_map/pool/ppermute | solution.py:185
  28.1 16.2 %copy-start = (s32[1,1,4,8]{3,2,1,0:T(4,128)S(1)}, s32[1,1,4,8]{3,2,1,0:T(4,128)}, u32[]{:S(2)}) copy-start(s32[1,1,4,8]{3,2,1,0:T(4,128)} %param.7) | copy-start | bytes 388
  44.9 8.8 %collective-permute-start.5 = (f32[4,64,128]{2,1,0:T(8,128)S(1)}, f32[4,64,128]{2,1,0:T(8,128)S(1)}, u32[]{:S(2)}, u32[]{:S(2)}) collective-permute-start(f32[4,64,128]{2,1,0:T(8,128)S(1)} %get-tuple-element.16.own), channel_id=1, source_target_pairs={{2,4},{3,5},{4,2},{5,3},{6,8},{7,9},{8,6},{9,7},{10,12},{11,13},{1... | collective-permute-start | bytes 393224 | tf_op jit(solution)/shard_map/halo/ppermute | solution.py:193
  45.5 8.1 %collective-permute-start.4 = (f32[4,64,128]{2,1,0:T(8,128)S(1)}, f32[4,64,128]{2,1,0:T(8,128)S(1)}, u32[]{:S(2)}, u32[]{:S(2)}) collective-permute-start(f32[4,64,128]{2,1,0:T(8,128)S(1)} %get-tuple-element.16.own), channel_id=1, source_target_pairs={{1,2},{2,1},{3,4},{4,3},{5,6},{6,5},{7,8},{8,7},{9,10},{10,9},{11,... | collective-permute-start | bytes 393224 | tf_op jit(solution)/shard_map/halo/ppermute | solution.py:192
  46.2 8.8 %collective-permute-start.3 = (f32[4,64,128]{2,1,0:T(8,128)S(1)}, f32[4,64,128]{2,1,0:T(8,128)S(1)}, u32[]{:S(2)}, u32[]{:S(2)}) collective-permute-start(f32[4,64,128]{2,1,0:T(8,128)S(1)} %get-tuple-element.16.own), channel_id=1, source_target_pairs={{0,2},{1,3},{2,0},{3,1},{4,6},{5,7},{6,4},{7,5},{8,10},{9,11},{10,... | collective-permute-start | bytes 393224 | tf_op jit(solution)/shard_map/halo/ppermute | solution.py:191
  51.7 6.9 %collective-permute-start.2 = (f32[4,64,128]{2,1,0:T(8,128)S(1)}, f32[4,64,128]{2,1,0:T(8,128)S(1)}, u32[]{:S(2)}, u32[]{:S(2)}) collective-permute-start(f32[4,64,128]{2,1,0:T(8,128)S(1)} %get-tuple-element.16.own), channel_id=1, source_target_pairs={{0,1},{1,0},{2,3},{3,2},{4,5},{5,4},{6,7},{7,6},{8,9},{9,8},{10,11... | collective-permute-start | bytes 393224 | tf_op jit(solution)/shard_map/halo/ppermute | solution.py:190
